TPU v7x, 128 devices: a whole 4x4x4 slice. The times are simulated.
128 devices in a mesh: expert: 128 (over x, y, z, core).
Axes of the slice: x: 4, y: 4, z: 4, core: 2. Of those that a mesh axis runs over, the one named last changes fastest.
Arguments:
- tokens: bfloat16 [16384, 3584], P('expert'), may hold values from -6 to 6
- cotangent: bfloat16 [16384, 3584], P('expert'), may hold values from -6 to 6
- routes: int32 [16384, 8], P('expert'), may hold values from 0 to 63, all different within a row; in each aligned block of 128 rows (0 to 127, 128 to 255, ...) at most 20 rows name the same one
- gates: bfloat16 [16384, 8], P('expert'), may hold values from 0.049804688 to 0.29882812
- previous_row: int32 [64], replicated, may hold values from 0 to 63, each once
- gu_payload: bfloat16 [64, 3584, 2048], P(None, 'expert'), may hold values from -0.09375 to 0.09375
- gu_scales: float32 [64, 28, 16], replicated, may hold values from 0.5 to 2
- down_payload: bfloat16 [64, 1024, 3584], P(None, 'expert'), may hold values from -0.1875 to 0.1875
- down_scales: float32 [64, 8, 28], replicated, may hold values from 0.5 to 2
Outputs:
- layer_out: bfloat16 [16384, 3584], P('expert')
- gate_grad: float32 [16384, 8], P('expert')
Inputs may be any that keep to these rules, and one draw needn't show every extreme that they name: `routes`: each token names 8 different experts; among the tokens of one device no expert is named by more than 20 of them, and in some devices' tokens one expert is named by exactly 20. `previous_row`: each stored row holds exactly one expert.
All inputs are finite; a program needn't handle non-finite values.
Results may differ from a plain program's by a relative error of at most 0.0076.
Values may be sent and summed in bfloat16 or wider, within the bound.
No kernel may reach another device: no remote copies, remote signals or barrier semaphores. Data moves between devices by JAX's collectives and lax.ppermute only.
A program may use at most 256 MiB of HBM per device.

v0:
```python
import jax
import jax.numpy as jnp
from jax import lax
from jax.sharding import PartitionSpec as P

FF = 1024
TOP = 8


def dequantize(payload, scales):
    expanded = jnp.repeat(jnp.repeat(scales, 128, axis=0), 128, axis=1)
    return (payload.astype(jnp.float32) * expanded).astype(jnp.bfloat16)


def shards(
    tokens, cotangent, routes, gates, previous_row, gu_payload, gu_scales, down_payload, down_scales
):
    model_width = tokens.shape[1]
    local_count = tokens.shape[0]
    devices = lax.axis_size("expert")
    device_id = lax.axis_index("expert")
    experts = previous_row.shape[0]
    source_rows = previous_row[jnp.arange(devices, dtype=jnp.int32) % experts]
    send_gate = jnp.take(gu_payload, source_rows, axis=0)
    send_down = jnp.take(down_payload, source_rows, axis=0)
    got_gate, got_down = (
        lax.all_to_all(send_gate, "expert", split_axis=0, concat_axis=0, tiled=True),
        lax.all_to_all(send_down, "expert", split_axis=0, concat_axis=0, tiled=True),
    )
    full_gate = got_gate.reshape(model_width, 2 * FF)
    full_down = got_down.reshape(FF, model_width)
    own_row = previous_row[device_id % experts]
    w_gu = dequantize(full_gate, gu_scales[own_row])
    w_down = dequantize(full_down, down_scales[own_row])
    flat_routes = routes.reshape(-1)
    route_count = flat_routes.shape[0]
    onehot = (flat_routes[:, None] == jnp.arange(experts, dtype=jnp.int32)[None, :]).astype(
        jnp.int32
    )
    route_rank = jnp.sum((jnp.cumsum(onehot, axis=0) - 1) * onehot, axis=1)
    most_rows = max(2, local_count * TOP * 5 // (4 * experts))
    capacity = (most_rows + 1) // 2
    second_host = route_rank >= capacity
    slot_index = jnp.where(second_host, route_rank - capacity, route_rank)
    target = flat_routes + experts * second_host.astype(jnp.int32)
    position = target * capacity + slot_index
    gather_table = (
        jnp.full((devices * capacity,), local_count, jnp.int32)
        .at[position]
        .set(jnp.arange(route_count, dtype=jnp.int32) // TOP)
    )
    outgoing = jnp.take(tokens, gather_table, axis=0, mode="fill", fill_value=0).reshape(
        devices, capacity, model_width
    )
    arrived = lax.all_to_all(outgoing, "expert", split_axis=0, concat_axis=0, tiled=True)
    row_block = arrived.reshape(-1, model_width)
    hidden = jnp.dot(row_block, w_gu, preferred_element_type=jnp.float32)
    active = (jax.nn.silu(hidden[:, :FF]) * hidden[:, FF:]).astype(jnp.bfloat16)
    result = jnp.dot(active, w_down, preferred_element_type=jnp.float32).astype(jnp.bfloat16)
    produced = result.reshape(arrived.shape)
    returned = lax.all_to_all(produced, "expert", split_axis=0, concat_axis=0, tiled=True)
    per_route = returned.reshape(-1, model_width)[position]
    stacked = per_route.reshape(local_count, TOP, model_width)
    layer_out = jnp.einsum("tk,tkd->td", gates, stacked, preferred_element_type=jnp.float32).astype(
        jnp.bfloat16
    )
    gate_grad = jnp.einsum("td,tkd->tk", cotangent, stacked, preferred_element_type=jnp.float32)
    return (layer_out, gate_grad)


def solution(mesh):
    in_specs = (
        P("expert", None),
        P("expert", None),
        P("expert", None),
        P("expert", None),
        P(),
        P(None, "expert", None),
        P(),
        P(None, "expert", None),
        P(),
    )
    out_specs = (P("expert", None), P("expert", None))
    return jax.shard_map(shards, mesh=mesh, in_specs=in_specs, out_specs=out_specs, check_vma=False)
```

profile of v0, /device:TPU:0, one launch (start us, length us, event | category | flops | bytes accessed | tf_op | source)
XLA Modules:
  0.0 930.7 jit_solution(2704885978229288119)
XLA Ops:
  0.6 0.0 copy-start
  0.6 0.9 copy.33
  1.5 0.1 eq.33
  1.6 0.1 eq.29
  1.7 0.1 reshape.170
  1.8 18.0 %reduce-window.6 = s32[64,8,128]{2,1,0:T(8,128)S(1)} reduce-window(s32[64,8,128]{2,1,0:T(8,128)S(1)} %fusion.16, s32[]{:T(128)} %constant.90.clone.1), window={size=1x1x128 pad=0_0x0_0x127_0}, to_apply=%region_0.1 | reduce-window | flops 8323072 | bytes 524292 | tf_op jit(solution)/shard_map/reduce-window
  19.8 0.1 slice.26
  20.0 0.1 copy.36
  20.2 0.1 copy.37
  20.2 0.1 add_add_fusion
  20.4 0.1 fusion.15
  20.5 0.0 copy-start.6
  20.5 4.3 scatter_custom_fusion
  24.9 0.0 copy-done
  24.9 7.9 gather_fusion
  32.8 0.0 copy-done.6
  32.8 14.2 %gather.23 = bf16[128,10,3584]{2,1,0:T(8,128)(2,1)} reshape(bf16[1280,3584]{1,0:T(8,128)(2,1)} %gather_fusion) | data formatting | bytes 18350080 | tf_op jit(solution)/shard_map/jit(_take)/gather | solution.py:52
  47.0 0.2 broadcast_in_dim.54
  47.2 10.9 %broadcast_select_fusion.1 = bf16[128,10,3584]{2,1,0:T(8,128)(2,1)} fusion(bf16[128,10,3584]{2,1,0:T(8,128)(2,1)} %gather.23, pred[128,10]{1,0:T(8,128)(4,1)S(1)} %broadcast_in_dim.54), kind=kLoop, calls=%fused_computation.14 | loop fusion | flops 4587520 | bytes 18351360 | tf_op jit(solution)/shard_map/jit(_take)/select_n | solution.py:52
  58.1 11.6 %all-to-all-start = ((bf16[128,10,3584]{2,1,0:T(8,128)(2,1)}), bf16[128,10,3584]{2,1,0:T(8,128)(2,1)}, u32[]{:S(2)}, u32[]{:S(2)}) async-start(bf16[128,10,3584]{2,1,0:T(8,128)(2,1)} %broadcast_select_fusion.1), calls=%async_computation | async-start | bytes 29360128 | tf_op jit(solution)/shard_map/all_to_all | solution.py:55
  69.7 0.0 copy-done.2
  69.7 1.2 gather_fusion.1
  71.0 33.0 %gather_fusion.2 = bf16[128,28,2048]{2,0,1:T(8,128)(2,1)} fusion(bf16[64,28,2048]{2,0,1:T(8,128)(2,1)} %param.14, s32[1024]{0:T(1024)S(1)} %pad_clamp_fusion.1), kind=kCustom, calls=%fused_computation.2 | custom fusion | bytes 29360640 | tf_op jit(solution)/shard_map/jit(_take)/gather | solution.py:24
  104.0 7.8 broadcast_select_fusion
  111.8 25.7 %copy.38 = bf16[128,28,2048]{2,1,0:T(8,128)(2,1)} copy(bf16[128,28,2048]{2,0,1:T(8,128)(2,1)S(1)} %broadcast_select_fusion) | data formatting | bytes 29360128 | tf_op jit(solution)/shard_map/jit(_take)/select_n | solution.py:24
  137.5 127.4 %all-to-all-done = bf16[128,10,3584]{2,1,0:T(8,128)(2,1)} async-done(((bf16[128,10,3584]{2,1,0:T(8,128)(2,1)}), bf16[128,10,3584]{2,1,0:T(8,128)(2,1)}, u32[]{:S(2)}, u32[]{:S(2)}) %all-to-all-start) | async-done | bytes 9175072 | tf_op jit(solution)/shard_map/all_to_all | solution.py:55
  264.9 14.9 %all-to-all-start.1 = ((bf16[128,28,2048]{2,1,0:T(8,128)(2,1)}), bf16[128,28,2048]{2,1,0:T(8,128)(2,1)}, u32[]{:S(2)}, u32[]{:S(2)}) async-start(bf16[128,28,2048]{2,1,0:T(8,128)(2,1)} %copy.38), calls=%async_computation.1 | async-start | bytes 33554432 | tf_op jit(solution)/shard_map/all_to_all | solution.py:27
  279.9 6.1 gather_fusion.3
  286.0 6.9 broadcast_select_fusion.2
  292.9 216.6 %all-to-all-done.1 = bf16[128,28,2048]{2,1,0:T(8,128)(2,1)} async-done(((bf16[128,28,2048]{2,1,0:T(8,128)(2,1)}), bf16[128,28,2048]{2,1,0:T(8,128)(2,1)}, u32[]{:S(2)}, u32[]{:S(2)}) %all-to-all-start.1) | async-done | bytes 14680096 | tf_op jit(solution)/shard_map/all_to_all | solution.py:27
  509.4 19.2 %all-to-all-start.2 = ((bf16[128,8,3584]{2,1,0:T(8,128)(2,1)}), bf16[128,8,3584]{2,1,0:T(8,128)(2,1)}, u32[]{:S(2)}, u32[]{:S(2)}) async-start(bf16[128,8,3584]{2,1,0:T(8,128)(2,1)} %broadcast_select_fusion.2), calls=%async_computation.2 | async-start | bytes 14680064 | tf_op jit(solution)/shard_map/all_to_all | solution.py:28
  528.6 0.6 dynamic_slice.9
  531.2 0.0 copy-done.4
  531.2 0.1 constant_dynamic-slice_fusion
  531.3 0.2 copy.50
  531.5 0.0 copy-done.5
  531.5 0.1 constant_dynamic-slice_fusion.1
  531.7 0.2 copy.51
  531.9 0.1 broadcast_bitcast_fusion
  532.1 7.1 broadcast_in_dim.65
  539.1 14.3 %copy.43 = f32[1024,3584]{1,0:T(8,128)} copy(f32[1024,3584]{0,1:T(8,128)} %bitcast.58) | data formatting | bytes 29360128 | tf_op jit(solution)/shard_map/reshape | solution.py:11
  553.4 14.6 %reshape.172 = bf16[1280,3584]{1,0:T(8,128)(2,1)} reshape(bf16[128,10,3584]{2,1,0:T(8,128)(2,1)} %all-to-all-done) | data formatting | bytes 18350080 | tf_op jit(solution)/shard_map/reshape | solution.py:56
  568.1 26.0 %reshape.179 = f32[3584,16,128]{2,1,0:T(8,128)} reshape(bf16[128,28,2048]{2,1,0:T(8,128)(2,1)} %all-to-all-done.1) | data formatting | bytes 44040192 | tf_op jit(solution)/shard_map/convert_element_type | solution.py:12
  594.0 0.1 broadcast_in_dim.60
  594.2 0.0 slice-start.1
  594.2 0.0 slice-start.2
  594.2 23.4 %multiply_convert_fusion = bf16[3584,16,128]{2,1,0:T(8,128)(2,1)} fusion(f32[3584,16,128]{2,1,0:T(8,128)} %reshape.179, f32[3584,16]{1,0:T(8,128)S(1)} %bitcast.62), kind=kLoop, calls=%fused_computation.6 | loop fusion | flops 14680064 | bytes 44269568 | tf_op jit(solution)/shard_map/convert_element_type | solution.py:12
  617.5 0.0 slice-done
  617.5 0.0 slice-done.1
  617.5 0.0 slice-done.2
  617.6 24.8 %fusion = f32[1280,2048]{1,0:T(8,128)} fusion(bf16[1280,3584]{1,0:T(8,128)(2,1)S(1)} %bitcast.61, bf16[448,8,16,128]{3,2,1,0:T(8,128)(2,1)} %bitcast.59), kind=kOutput, calls=%fused_computation.8 | convolution fusion | flops 18790481920 | bytes 34340864 | tf_op jit(solution)/shard_map/dot_general | solution.py:57
  642.4 0.0 all-to-all-done.2
  642.4 21.2 %convolution_convert_fusion = bf16[1280,3584]{1,0:T(8,128)(2,1)} fusion(f32[1024,3584]{1,0:T(8,128)} %copy.43, bf16[128,8,3584]{2,1,0:T(8,128)(2,1)} %all-to-all-done.2, f32[1280,2048]{1,0:T(8,128)} %fusion), kind=kOutput, calls=%fused_computation.7 | convolution fusion | flops 9418702848 | bytes 41680896 | tf_op jit(solution)/shard_map/dot_general | solution.py:59
  663.6 14.2 %reshape.176 = bf16[128,10,3584]{2,1,0:T(8,128)(2,1)} reshape(bf16[1280,3584]{1,0:T(8,128)(2,1)} %convolution_convert_fusion) | data formatting | bytes 18350080 | tf_op jit(solution)/shard_map/reshape | solution.py:60
  677.8 10.2 %all-to-all-start.3 = ((bf16[128,10,3584]{2,1,0:T(8,128)(2,1)}), bf16[128,10,3584]{2,1,0:T(8,128)(2,1)}, u32[]{:S(2)}, u32[]{:S(2)}) async-start(bf16[128,10,3584]{2,1,0:T(8,128)(2,1)} %reshape.176), calls=%async_computation.3 | async-start | bytes 29360128 | tf_op jit(solution)/shard_map/all_to_all | solution.py:61
  688.0 0.1 copy.44
  688.2 195.1 %all-to-all-done.3 = bf16[128,10,3584]{2,1,0:T(8,128)(2,1)} async-done(((bf16[128,10,3584]{2,1,0:T(8,128)(2,1)}), bf16[128,10,3584]{2,1,0:T(8,128)(2,1)}, u32[]{:S(2)}, u32[]{:S(2)}) %all-to-all-start.3) | async-done | bytes 9175072 | tf_op jit(solution)/shard_map/all_to_all | solution.py:61
  883.3 14.6 %reshape.177 = bf16[1280,3584]{1,0:T(8,128)(2,1)} reshape(bf16[128,10,3584]{2,1,0:T(8,128)(2,1)} %all-to-all-done.3) | data formatting | bytes 18350080 | tf_op jit(solution)/shard_map/reshape | solution.py:62
  897.9 18.6 %gather_fusion.4 = bf16[1024,3584]{1,0:T(8,128)(2,1)} fusion(bf16[1280,3584]{1,0:T(8,128)(2,1)} %reshape.177, s32[1024]{0:T(1024)S(1)} %broadcast_clamp_fusion), kind=kCustom, calls=%fused_computation.4 | custom fusion | bytes 14684160 | tf_op jit(solution)/shard_map/gather | solution.py:62
  916.5 6.6 fusion.8
  923.1 2.6 copy.63
  925.7 0.0 copy-done.3
  925.7 4.1 fusion.6
  929.8 0.7 copy.47
  (30 shorter events, 0.2 us)
Async XLA Ops:
  0.6 24.2 %copy-start = (bf16[128,3584]{1,0:T(8,128)(2,1)S(1)}, bf16[128,3584]{1,0:T(8,128)(2,1)}, u32[]{:S(2)}) copy-start(bf16[128,3584]{1,0:T(8,128)(2,1)} %param.9) | copy-start | bytes 2752516
  20.5 12.3 %copy-start.6 = (s32[1024,1]{0,1:T(1,128)}, s32[1024,1]{0,1:T(1,128)S(1)}, u32[]{:S(2)}) copy-start(s32[1024,1]{0,1:T(1,128)S(1)} %compare_select_fusion) | copy-start | bytes 12292
  58.1 11.6 %copy-start.2 = (s32[64]{0:T(128)S(1)}, s32[64]{0:T(128)}, u32[]{:S(2)}) copy-start(s32[64]{0:T(128)} %param.13) | copy-start | bytes 772
  58.1 206.9 %all-to-all-start = ((bf16[128,10,3584]{2,1,0:T(8,128)(2,1)}), bf16[128,10,3584]{2,1,0:T(8,128)(2,1)}, u32[]{:S(2)}, u32[]{:S(2)}) async-start(bf16[128,10,3584]{2,1,0:T(8,128)(2,1)} %broadcast_select_fusion.1), calls=%async_computation | async-start | bytes 29360128 | tf_op jit(solution)/shard_map/all_to_all | solution.py:55
  264.9 244.5 %all-to-all-start.1 = ((bf16[128,28,2048]{2,1,0:T(8,128)(2,1)}), bf16[128,28,2048]{2,1,0:T(8,128)(2,1)}, u32[]{:S(2)}, u32[]{:S(2)}) async-start(bf16[128,28,2048]{2,1,0:T(8,128)(2,1)} %copy.38), calls=%async_computation.1 | async-start | bytes 33554432 | tf_op jit(solution)/shard_map/all_to_all | solution.py:27
  292.9 238.3 %copy-start.4 = (f32[64,28,16]{0,2,1:T(8,128)S(1)}, f32[64,28,16]{0,2,1:T(8,128)}, u32[]{:S(2)}) copy-start(f32[64,28,16]{0,2,1:T(8,128)} %param.15) | copy-start | bytes 344068
  292.9 238.7 %copy-start.5 = (f32[64,8,28]{0,1,2:T(8,128)S(1)}, f32[64,8,28]{0,1,2:T(8,128)}, u32[]{:S(2)}) copy-start(f32[64,8,28]{0,1,2:T(8,128)} %param.17) | copy-start | bytes 172036
  509.4 133.0 %all-to-all-start.2 = ((bf16[128,8,3584]{2,1,0:T(8,128)(2,1)}), bf16[128,8,3584]{2,1,0:T(8,128)(2,1)}, u32[]{:S(2)}, u32[]{:S(2)}) async-start(bf16[128,8,3584]{2,1,0:T(8,128)(2,1)} %broadcast_select_fusion.2), calls=%async_computation.2 | async-start | bytes 14680064 | tf_op jit(solution)/shard_map/all_to_all | solution.py:28
  594.0 23.5 %slice-start = ((s8[9175040]{0:T(1024)(128)(4,1)}), s8[4194304]{0:T(1024)(128)(4,1)S(1)}, s32[]{:S(2)}) async-start(s8[9175040]{0:T(1024)(128)(4,1)} %bitcast.60), calls=%async_computation.4 | async-start | bytes 8388608
  594.2 23.4 %slice-start.1 = ((s8[9175040]{0:T(1024)(128)(4,1)}), s8[4194304]{0:T(1024)(128)(4,1)S(1)}, s32[]{:S(2)}) async-start(s8[9175040]{0:T(1024)(128)(4,1)} %bitcast.60), calls=%async_computation.5 | async-start | bytes 8388608
  594.2 23.4 %slice-start.2 = ((s8[9175040]{0:T(1024)(128)(4,1)}), s8[786432]{0:T(1024)(128)(4,1)S(1)}, s32[]{:S(2)}) async-start(s8[9175040]{0:T(1024)(128)(4,1)} %bitcast.60), calls=%async_computation.6 | async-start | bytes 1572864
  677.8 10.2 %copy-start.8 = (bf16[128,8]{0,1:T(8,128)(2,1)S(1)}, bf16[128,8]{0,1:T(8,128)(2,1)}, u32[]{:S(2)}) copy-start(bf16[128,8]{0,1:T(8,128)(2,1)} %param.12) | copy-start | bytes 6148
  677.8 10.3 %copy-start.7 = (s32[1024,1]{0,1:T(1,128)S(1)}, s32[1024,1]{0,1:T(1,128)}, u32[]{:S(2)}) copy-start(s32[1024,1]{0,1:T(1,128)} %copy-done.6) | copy-start | bytes 12292
  677.8 205.4 %all-to-all-start.3 = ((bf16[128,10,3584]{2,1,0:T(8,128)(2,1)}), bf16[128,10,3584]{2,1,0:T(8,128)(2,1)}, u32[]{:S(2)}, u32[]{:S(2)}) async-start(bf16[128,10,3584]{2,1,0:T(8,128)(2,1)} %reshape.176), calls=%async_computation.3 | async-start | bytes 29360128 | tf_op jit(solution)/shard_map/all_to_all | solution.py:61
  916.5 9.2 copy-start.3
  916.5 9.2 copy-start.9
  923.1 7.4 copy-start.1
where the time goes:
time: 945 us; the launch traced here: 931 us
  waiting for transfers between devices  539 us (57%)
  local copies, waits for them, and re-layouts  209 us (22%)
  other arithmetic  67.2 us (7%)
  matrix products  56.8 us (6%)
  starting transfers between devices  55.9 us (6%)
    all_to_all x1, waiting for transfers between devices, shards(): lax.all_to_all(send_gate, 'expert', split_axis=0, concat_axis=0, tiled=True)  217 us
    all_to_all x1, waiting for transfers between devices, shards(): lax.all_to_all(produced, 'expert', split_axis=0, concat_axis=0, tiled=True)  195 us
    all_to_all x1, waiting for transfers between devices, shards(): lax.all_to_all(outgoing, 'expert', split_axis=0, concat_axis=0, tiled=True)  127 us
    gather x1, local copies, waits for them, and re-layouts, shards(): send_gate = jnp.take(gu_payload, source_rows, axis=0)  33 us
    convert_element_type x1, local copies, waits for them, and re-layouts, dequantize(): return (payload.astype(jnp.float32) * expanded).astype(jnp.bfloat16)  26 us
    select_n x1, local copies, waits for them, and re-layouts, shards(): send_gate = jnp.take(gu_payload, source_rows, axis=0)  25.7 us
    dot_general x1, matrix products, shards(): hidden = jnp.dot(row_block, w_gu, preferred_element_type=jnp.float32)  24.8 us
    convert_element_type x1, other arithmetic, dequantize(): return (payload.astype(jnp.float32) * expanded).astype(jnp.bfloat16)  23.4 us
  transfers between devices with their start and end apart: 4, of which 3 were waited for; matrix products, arithmetic and copies ran while one was open for 21% of the time, Pallas kernels for 0%

commit v1 on v0

v1 whole, which is shorter than its diff:
```python
import jax
import jax.numpy as jnp
from jax import lax
from jax.experimental import pallas as pl
from jax.experimental.pallas import tpu as pltpu
from jax.sharding import PartitionSpec as P

FF = 1024
TOP = 8
MOST = 20
FIRST = 16


def gu_kernel(parity_ref, own_ref, other_ref, scale_ref, out_ref):
    step = pl.program_id(0)
    width = out_ref.shape[1]
    even_core = parity_ref[0] == 0
    parts = []
    for chip in range(own_ref.shape[0]):
        own = own_ref[chip].astype(jnp.float32)
        other = other_ref[chip].astype(jnp.float32)
        for rows in (jnp.where(even_core, own, other), jnp.where(even_core, other, own)):
            parts += [rows[:, g * width : (g + 1) * width] for g in range(3)]
            fold = rows[:, 3 * width :]
            parts.append(jnp.concatenate([fold[:4], fold[4:]], axis=1))
    values = jnp.concatenate(parts, axis=0)
    count = values.shape[0]
    low = (step * count) // 128
    high = jnp.minimum(low + 1, scale_ref.shape[0] - 1)
    row = step * count + lax.broadcasted_iota(jnp.int32, values.shape, 0)
    scale = jnp.where(row < 128 * (low + 1), scale_ref[pl.ds(low, 1), :], scale_ref[pl.ds(high, 1), :])
    out_ref[...] = (values * scale).astype(jnp.bfloat16)


def dequantize_gu(own, other, scales, parity):
    chips, _, packed = own.shape
    width = packed * 2 // 7
    return pl.pallas_call(
        gu_kernel,
        grid=(chips // 2,),
        in_specs=[
            pl.BlockSpec(memory_space=pltpu.SMEM),
            pl.BlockSpec((2, 8, packed), lambda i: (i, 0, 0)),
            pl.BlockSpec((2, 8, packed), lambda i: (i, 0, 0)),
            pl.BlockSpec(scales.shape, lambda i: (0, 0)),
        ],
        out_specs=pl.BlockSpec((112, width), lambda i: (i, 0)),
        out_shape=jax.ShapeDtypeStruct((chips * 56, width), jnp.bfloat16),
        compiler_params=pltpu.CompilerParams(vmem_limit_bytes=32 * 1024 * 1024),
        cost_estimate=pl.CostEstimate(flops=chips * 56 * width, bytes_accessed=chips * 56 * width * 4, transcendentals=0),
        name="dequantize_gu",
    )(parity, own, other, scales)


def down_kernel(parity_ref, own_ref, other_ref, scale_ref, out_ref):
    step = pl.program_id(0)
    even_core = parity_ref[0] == 0
    parts = []
    for chip in range(own_ref.shape[0]):
        own = own_ref[chip].astype(jnp.float32)
        other = other_ref[chip].astype(jnp.float32)
        parts += [jnp.where(even_core, own, other), jnp.where(even_core, other, own)]
    values = jnp.concatenate(parts, axis=0)
    scale = scale_ref[pl.ds(step * values.shape[0] // 128, 1), :]
    out_ref[...] = (values * scale).astype(jnp.bfloat16)


def dequantize_down(own, other, scales, parity):
    chips, _, width = own.shape
    return pl.pallas_call(
        down_kernel,
        grid=(chips // 4,),
        in_specs=[
            pl.BlockSpec(memory_space=pltpu.SMEM),
            pl.BlockSpec((4, 8, width), lambda i: (i, 0, 0)),
            pl.BlockSpec((4, 8, width), lambda i: (i, 0, 0)),
            pl.BlockSpec(scales.shape, lambda i: (0, 0)),
        ],
        out_specs=pl.BlockSpec((64, width), lambda i: (i, 0)),
        out_shape=jax.ShapeDtypeStruct((chips * 16, width), jnp.bfloat16),
        compiler_params=pltpu.CompilerParams(vmem_limit_bytes=32 * 1024 * 1024),
        cost_estimate=pl.CostEstimate(flops=chips * 16 * width, bytes_accessed=chips * 16 * width * 4, transcendentals=0),
        name="dequantize_down",
    )(parity, own, other, scales)


def shards(
    tokens, cotangent, routes, gates, previous_row, gu_payload, gu_scales, down_payload, down_scales
):
    local_count, model_width = tokens.shape
    devices = lax.axis_size("expert")
    experts = previous_row.shape[0]
    device_id = lax.axis_index("expert")
    chip, core = device_id // 2, device_id % 2
    parity = core.astype(jnp.int32).reshape(1)
    same_core = [[2 * c + p for c in range(experts)] for p in range(2)]
    swap = [(d, d ^ 1) for d in range(devices)]

    def exchange(x):
        return lax.all_to_all(x, "expert", 0, 0, axis_index_groups=same_core, tiled=True)

    down_own = exchange(down_payload)
    down_other = lax.ppermute(down_own, "expert", swap)

    packed_gu = jnp.concatenate(
        [gu_payload[:, 8 * g : 8 * g + 8] for g in range(3)]
        + [jnp.concatenate([gu_payload[:, 24:28, :FF], gu_payload[:, 24:28, FF:]], axis=1)],
        axis=2,
    )
    packed_gu, down_own = lax.optimization_barrier((packed_gu, down_own))
    gu_own = exchange(packed_gu)
    gu_other = lax.ppermute(gu_own, "expert", swap)

    routes_t = routes.T
    gates_t = gates.T.astype(jnp.float32)
    slots = jnp.arange(experts, dtype=jnp.int32)[None, :, None]
    target = jnp.sum(
        jnp.where(routes_t[:, None, :] == slots, previous_row[None, :, None], 0), axis=1
    )
    named = target[:, None, :] == slots
    member = jnp.any(named, axis=0)
    gate_of = jnp.sum(jnp.where(named, gates_t[:, None, :], 0.0), axis=0)
    earlier = jnp.arange(local_count)[:, None] < jnp.arange(local_count)[None, :]
    rank = jnp.dot(
        member.astype(jnp.bfloat16), earlier.astype(jnp.bfloat16), preferred_element_type=jnp.float32
    ).astype(jnp.int32)
    rank = jnp.where(member, rank, -1)

    w_down = dequantize_down(
        down_own, down_other, jnp.repeat(down_scales[chip], 128, axis=1), parity
    )
    w_gu = dequantize_gu(gu_own, gu_other, jnp.repeat(gu_scales[chip], 128, axis=1), parity)

    def chosen(start, count):
        places = jnp.arange(start, start + count, dtype=jnp.int32)[None, :, None]
        return rank[:, None, :] == places

    def dispatch(start, count, after):
        select = chosen(start, count).reshape(experts * count, local_count).astype(jnp.bfloat16)
        outgoing = jnp.dot(select, tokens, preferred_element_type=jnp.float32).astype(jnp.bfloat16)
        outgoing = outgoing.reshape(experts, count, model_width)
        outgoing, after = lax.optimization_barrier((outgoing, after))
        return exchange(outgoing), after

    def expert(arrived):
        rows = arrived.reshape(-1, model_width)
        hidden = jnp.dot(rows, w_gu, preferred_element_type=jnp.float32)
        active = (jax.nn.silu(hidden[:, :FF]) * hidden[:, FF:]).astype(jnp.bfloat16)
        result = jnp.dot(active, w_down, preferred_element_type=jnp.float32).astype(jnp.bfloat16)
        return result.reshape(arrived.shape)

    def combine(returned, start, count):
        mask = chosen(start, count)
        rows = returned.reshape(-1, model_width)
        weight = jnp.where(mask, gate_of[:, None, :], 0.0).astype(jnp.bfloat16)
        summed = lax.dot_general(
            weight.reshape(-1, local_count),
            rows,
            (((0,), (0,)), ((), ())),
            preferred_element_type=jnp.float32,
        )
        inner = lax.dot_general(
            rows, cotangent, (((1,), (1,)), ((), ())), preferred_element_type=jnp.float32
        ).reshape(mask.shape)
        return summed, jnp.sum(jnp.where(mask, inner, 0.0), axis=1)

    rest = MOST - FIRST
    arrived_a, gu_own = dispatch(0, FIRST, gu_own)
    arrived_b, arrived_a = dispatch(FIRST, rest, arrived_a)
    produced_a = expert(arrived_a)
    produced_a, arrived_b = lax.optimization_barrier((produced_a, arrived_b))
    returned_a = exchange(produced_a)
    produced_b = expert(arrived_b)
    produced_b, returned_a = lax.optimization_barrier((produced_b, returned_a))
    returned_b = exchange(produced_b)
    out_a, grad_a = combine(returned_a, 0, FIRST)
    out_b, grad_b = combine(returned_b, FIRST, rest)
    layer_out = (out_a + out_b).astype(jnp.bfloat16)
    grad = grad_a + grad_b
    gate_grad = jnp.sum(jnp.where(named, grad[None], 0.0), axis=1).T
    return (layer_out, gate_grad)


def solution(mesh):
    in_specs = (
        P("expert", None),
        P("expert", None),
        P("expert", None),
        P("expert", None),
        P(),
        P(None, "expert", None),
        P(),
        P(None, "expert", None),
        P(),
    )
    out_specs = (P("expert", None), P("expert", None))
    return jax.shard_map(shards, mesh=mesh, in_specs=in_specs, out_specs=out_specs, check_vma=False)
```

time: 945 us -> 525 us (0.56); the launches traced: 931 us -> 524 us
  waiting for transfers between devices: 539 us -> 313 us
  local copies, waits for them, and re-layouts: 209 us -> 24.8 us
  other arithmetic: 67.2 us -> 5.02 us
  Pallas kernels: 0 us -> 35.6 us
  starting transfers between devices: 55.9 us -> 85.9 us
    all_to_all x4 -> x6, waiting for transfers between devices: 539 us -> 309 us  [exchange(): lax.all_to_all(x, 'expert', 0, 0, axis_index_groups=same_core, tiled=True)]
    gather x6 -> x0, local copies, waits for them, and re-layouts: 81 us -> none  [the longest x1 33 us: shards(): send_gate = jnp.take(gu_payload, source_rows, axis=0)]
    reshape x5 -> x4, local copies, waits for them, and re-layouts: 57.9 us -> 9.83 us  [the longest x1 4.16 us: expert(): return result.reshape(arrived.shape)]
    pallas_call x0 -> x2, Pallas kernels: none -> 35.6 us  [the longest x1 25.5 us: dequantize_gu(): pl.pallas_call(gu_kernel, grid=(chips // 2,), in_specs=[pl.BlockSpec(memo...]
    all_to_all x4 -> x6, starting transfers between devices: 55.9 us -> 85.4 us  [exchange(): lax.all_to_all(x, 'expert', 0, 0, axis_index_groups=same_core, tiled=True)]
    convert_element_type x1 -> x0, local copies, waits for them, and re-layouts: 26 us -> none  [dequantize(): return (payload.astype(jnp.float32) * expanded).astype(jnp.bfloat16)]
    select_n x1 -> x0, local copies, waits for them, and re-layouts: 25.7 us -> none  [shards(): send_gate = jnp.take(gu_payload, source_rows, axis=0)]
    select_n x8 -> x0, other arithmetic: 25.6 us -> none  [the longest x2 10.9 us: shards(): jnp.take(tokens, gather_table, axis=0, mode='fill', fill_value=0)]
  transfers between devices with their start and end apart: 4 -> 8, of which waited for: 3 -> 6; matrix products, arithmetic and copies ran while one was open for 21% -> 15% of each run, Pallas kernels for 0% -> 7%
where the time goes in v1:
time: 525 us; the launch traced here: 524 us
  waiting for transfers between devices  313 us (60%)
  starting transfers between devices  85.9 us (16%)
  matrix products  58.7 us (11%)
  Pallas kernels  35.6 us (7%)
  local copies, waits for them, and re-layouts  24.8 us (5%)
    all_to_all x6, waiting for transfers between devices, exchange(): lax.all_to_all(x, 'expert', 0, 0, axis_index_groups=same_core, tiled=True)  309 us
    all_to_all x6, starting transfers between devices, exchange(): lax.all_to_all(x, 'expert', 0, 0, axis_index_groups=same_core, tiled=True)  85.4 us
    dot_general x2, matrix products, expert(): hidden = jnp.dot(rows, w_gu, preferred_element_type=jnp.float32)  28.1 us
    pallas_call x1, Pallas kernels, dequantize_gu(): pl.pallas_call(gu_kernel, grid=(chips // 2,), in_specs=[pl.BlockSpec(memo...  25.5 us
    dot_general x2, matrix products, expert(): jnp.dot(active, w_down, preferred_element_type=jnp.float32)  13.3 us
  transfers between devices with their start and end apart: 8, of which 6 were waited for; matrix products, arithmetic and copies ran while one was open for 15% of the time, Pallas kernels for 7%

profile of v1, /device:TPU:0, one launch (start us, length us, event | category | flops | bytes accessed | tf_op | source)
XLA Modules:
  0.0 523.6 jit_solution(8166275007424500964)
XLA Ops:
  0.6 0.0 copy-start
  0.6 11.9 %all-to-all-start = ((bf16[64,8,3584]{2,1,0:T(8,128)(2,1)}), bf16[64,8,3584]{2,1,0:T(8,128)(2,1)}, u32[]{:S(2)}, u32[]{:S(2)}) async-start(bf16[64,8,3584]{2,1,0:T(8,128)(2,1)} %param.16), calls=%async_computation | async-start | bytes 7340032 | tf_op jit(solution)/shard_map/all_to_all | solution.py:100
  12.5 4.0 fusion.37
  16.5 1.2 copy.56
  17.7 1.2 copy.57
  18.8 1.2 copy.58
  20.0 1.3 fusion.38
  21.3 0.4 copy.59
  21.7 0.4 copy.60
  22.1 4.0 maximum_maximum_fusion
  26.1 32.8 %all-to-all-done.own_ref = bf16[64,8,3584]{2,1,0:T(8,128)(2,1)} async-done(((bf16[64,8,3584]{2,1,0:T(8,128)(2,1)}), bf16[64,8,3584]{2,1,0:T(8,128)(2,1)}, u32[]{:S(2)}, u32[]{:S(2)}) %all-to-all-start) | async-done | bytes 3670048 | tf_op jit(solution)/shard_map/all_to_all | solution.py:100
  59.0 12.2 %all-to-all-start.1 = ((bf16[64,8,7168]{2,1,0:T(8,128)(2,1)}), bf16[64,8,7168]{2,1,0:T(8,128)(2,1)}, u32[]{:S(2)}, u32[]{:S(2)}) async-start(bf16[64,8,7168]{2,1,0:T(8,128)(2,1)} %maximum_maximum_fusion), calls=%async_computation.1 | async-start | bytes 14680064 | tf_op jit(solution)/shard_map/all_to_all | solution.py:100
  71.2 0.1 eq.107
  71.3 0.0 copy-done.6
  71.3 0.0 copy-done.8
  71.3 0.1 select_reduce_fusion.2
  71.4 0.1 fusion.15
  71.6 0.2 bitcast_compare_fusion
  71.8 94.7 %all-to-all-done.1.own_ref = bf16[64,8,7168]{2,1,0:T(8,128)(2,1)} async-done(((bf16[64,8,7168]{2,1,0:T(8,128)(2,1)}), bf16[64,8,7168]{2,1,0:T(8,128)(2,1)}, u32[]{:S(2)}, u32[]{:S(2)}) %all-to-all-start.1) | async-done | bytes 7340064 | tf_op jit(solution)/shard_map/all_to_all | solution.py:100
  166.5 0.0 collective-permute-start
  166.5 0.0 copy-done
  166.5 5.0 convolution_convert_fusion.1
  171.5 18.2 %all-to-all-start.2 = ((bf16[64,16,3584]{2,1,0:T(8,128)(2,1)}), bf16[64,16,3584]{2,1,0:T(8,128)(2,1)}, u32[]{:S(2)}, u32[]{:S(2)}) async-start(bf16[64,16,3584]{2,1,0:T(8,128)(2,1)} %bitcast.50), calls=%async_computation.2 | async-start | bytes 14680064 | tf_op jit(solution)/shard_map/all_to_all | solution.py:100
  189.7 0.5 collective-permute-start.1
  190.2 0.0 copy-done.4
  190.2 0.1 constant_dynamic-slice_fusion
  190.3 0.0 copy-start.5
  190.4 0.2 copy.64
  190.6 0.1 broadcast_in_dim.97
  190.8 0.1 copy.66
  190.9 0.1 eq.102
  191.0 0.7 convolution_convert_fusion.3
  191.7 1.4 reshape.62
  193.1 0.0 copy-done.5
  193.1 0.1 constant_dynamic-slice_fusion.1
  193.2 0.2 copy.65
  193.5 0.1 broadcast_bitcast_fusion.scale_ref
  193.6 3.1 collective-permute-done.1.other_ref
  196.7 10.1 %dequantize_down.1 = bf16[1024,3584]{1,0:T(8,128)(2,1)S(1)} custom-call(s32[1]{0:T(128)} %bitcast.6.parity_ref, bf16[64,8,3584]{2,1,0:T(8,128)(2,1)} %all-to-all-done.own_ref, bf16[64,8,3584]{2,1,0:T(8,128)(2,1)} %collective-permute-done.1.other_ref, f32[8,3584]{1,0:T(8,128)S(1)} %broadcast_bitcast_fusion.scale_ref), custom_call_target="tpu_custom_call" | custom-call | flops 3670016 | bytes 14680064 | tf_op jit(solution)/shard_map/dequantize_down/pallas_call | solution.py:70
  206.9 2.9 copy-done.2
  209.8 86.7 %all-to-all-done.2 = bf16[64,16,3584]{2,1,0:T(8,128)(2,1)} async-done(((bf16[64,16,3584]{2,1,0:T(8,128)(2,1)}), bf16[64,16,3584]{2,1,0:T(8,128)(2,1)}, u32[]{:S(2)}, u32[]{:S(2)}) %all-to-all-start.2) | async-done | bytes 7340064 | tf_op jit(solution)/shard_map/all_to_all | solution.py:100
  296.5 15.7 %all-to-all-start.3 = ((bf16[64,4,3584]{2,1,0:T(4,128)(2,1)}), bf16[64,4,3584]{2,1,0:T(4,128)(2,1)S(1)}, u32[]{:S(2)}, u32[]{:S(2)}) async-start(bf16[64,4,3584]{2,1,0:T(4,128)(2,1)} %reshape.62), calls=%async_computation.3 | async-start | bytes 3670016 | tf_op jit(solution)/shard_map/all_to_all | solution.py:100
  312.2 0.0 collective-permute-done.other_ref
  312.2 0.0 slice-start
  312.2 25.5 %dequantize_gu.1 = bf16[3584,2048]{1,0:T(8,128)(2,1)} custom-call(s32[1]{0:T(128)} %bitcast.6.parity_ref, bf16[64,8,7168]{2,1,0:T(8,128)(2,1)} %all-to-all-done.1.own_ref, bf16[64,8,7168]{2,1,0:T(8,128)(2,1)} %collective-permute-done.other_ref, f32[28,2048]{1,0:T(8,128)S(1)} %bitcast.49), custom_call_target="tpu_custom_call" | custom-call | flops 7340032 | bytes 29360128 | tf_op jit(solution)/shard_map/dequantize_gu/pallas_call | solution.py:38
  337.7 20.2 %fusion.39 = f32[1024,2048]{1,0:T(8,128)S(1)} fusion(bf16[1024,3584]{1,0:T(8,128)(2,1)} %bitcast.5, bf16[3584,2048]{1,0:T(8,128)(2,1)} %dequantize_gu.1), kind=kOutput, calls=%fused_computation.58 | convolution fusion | flops 15032385536 | bytes 30408704 | tf_op jit(solution)/shard_map/dot_general | solution.py:147
  357.9 9.9 %convolution_convert_fusion = bf16[1024,3584]{1,0:T(8,128)(2,1)} fusion(bf16[1024,3584]{1,0:T(8,128)(2,1)S(1)} %bitcast.46, f32[1024,2048]{1,0:T(8,128)S(1)} %fusion.39), kind=kOutput, calls=%fused_computation | convolution fusion | flops 7526154240 | bytes 23068672 | tf_op jit(solution)/shard_map/dot_general | solution.py:149
  367.8 0.0 all-to-all-done.3
  367.8 1.3 copy-done.3
  369.1 10.6 %all-to-all-start.4 = ((bf16[64,16,3584]{2,1,0:T(8,128)(2,1)}), bf16[64,16,3584]{2,1,0:T(8,128)(2,1)}, u32[]{:S(2)}, u32[]{:S(2)}) async-start(bf16[64,16,3584]{2,1,0:T(8,128)(2,1)} %bitcast.51), calls=%async_computation.4 | async-start | bytes 14680064 | tf_op jit(solution)/shard_map/all_to_all | solution.py:100
  379.7 0.0 slice-start.2
  379.7 4.1 reshape.69
  383.8 7.9 %fusion.40 = f32[256,2048]{1,0:T(8,128)S(1)} fusion(bf16[256,3584]{1,0:T(8,128)(2,1)} %reshape.69, bf16[3584,2048]{1,0:T(8,128)(2,1)} %dequantize_gu.1), kind=kOutput, calls=%fused_computation.59 | convolution fusion | flops 3758096384 | bytes 18612224 | tf_op jit(solution)/shard_map/dot_general | solution.py:147
  391.8 3.3 convolution_convert_fusion.2
  395.1 4.2 reshape.70
  399.3 77.0 %all-to-all-done.4 = bf16[64,16,3584]{2,1,0:T(8,128)(2,1)} async-done(((bf16[64,16,3584]{2,1,0:T(8,128)(2,1)}), bf16[64,16,3584]{2,1,0:T(8,128)(2,1)}, u32[]{:S(2)}, u32[]{:S(2)}) %all-to-all-start.4) | async-done | bytes 7340064 | tf_op jit(solution)/shard_map/all_to_all | solution.py:100
  476.3 16.9 %all-to-all-start.5 = ((bf16[64,4,3584]{2,1,0:T(4,128)(2,1)}), bf16[64,4,3584]{2,1,0:T(4,128)(2,1)S(1)}, u32[]{:S(2)}, u32[]{:S(2)}) async-start(bf16[64,4,3584]{2,1,0:T(4,128)(2,1)} %reshape.70), calls=%async_computation.5 | async-start | bytes 3670016 | tf_op jit(solution)/shard_map/all_to_all | solution.py:100
  493.2 0.0 copy-done.7
  493.2 5.1 fusion.8
  498.4 18.1 %all-to-all-done.5 = bf16[64,4,3584]{2,1,0:T(4,128)(2,1)S(1)} async-done(((bf16[64,4,3584]{2,1,0:T(4,128)(2,1)}), bf16[64,4,3584]{2,1,0:T(4,128)(2,1)S(1)}, u32[]{:S(2)}, u32[]{:S(2)}) %all-to-all-start.5) | async-done | bytes 1835040 | tf_op jit(solution)/shard_map/all_to_all | solution.py:100
  516.5 0.6 fusion.12
  517.2 0.6 select_reduce_fusion
  517.8 0.6 convolution_bitcast_fusion
  518.4 5.2 fusion.1
  (26 shorter events, 0.1 us)
Async XLA Ops:
  0.6 165.9 %copy-start = (bf16[128,3584]{1,0:T(8,128)(2,1)S(1)}, bf16[128,3584]{1,0:T(8,128)(2,1)}, u32[]{:S(2)}) copy-start(bf16[128,3584]{1,0:T(8,128)(2,1)} %param.9) | copy-start | bytes 2752516
  0.6 58.3 %all-to-all-start = ((bf16[64,8,3584]{2,1,0:T(8,128)(2,1)}), bf16[64,8,3584]{2,1,0:T(8,128)(2,1)}, u32[]{:S(2)}, u32[]{:S(2)}) async-start(bf16[64,8,3584]{2,1,0:T(8,128)(2,1)} %param.16), calls=%async_computation | async-start | bytes 7340032 | tf_op jit(solution)/shard_map/all_to_all | solution.py:100
  26.1 45.1 %copy-start.6 = (s32[128,8]{0,1:T(8,128)S(1)}, s32[128,8]{0,1:T(8,128)}, u32[]{:S(2)}) copy-start(s32[128,8]{0,1:T(8,128)} %param.11) | copy-start | bytes 12292
  26.1 45.1 %copy-start.8 = (s32[64]{0:T(128)S(1)}, s32[64]{0:T(128)}, u32[]{:S(2)}) copy-start(s32[64]{0:T(128)} %param.13) | copy-start | bytes 772
  59.0 107.5 %all-to-all-start.1 = ((bf16[64,8,7168]{2,1,0:T(8,128)(2,1)}), bf16[64,8,7168]{2,1,0:T(8,128)(2,1)}, u32[]{:S(2)}, u32[]{:S(2)}) async-start(bf16[64,8,7168]{2,1,0:T(8,128)(2,1)} %maximum_maximum_fusion), calls=%async_computation.1 | async-start | bytes 14680064 | tf_op jit(solution)/shard_map/all_to_all | solution.py:100
  166.5 145.7 %collective-permute-start = (bf16[64,8,7168]{2,1,0:T(8,128)(2,1)}, bf16[64,8,7168]{2,1,0:T(8,128)(2,1)}, u32[]{:S(2)}, u32[]{:S(2)}) collective-permute-start(bf16[64,8,7168]{2,1,0:T(8,128)(2,1)} %all-to-all-done.1.own_ref), channel_id=1, source_target_pairs={{0,1},{1,0},{2,3},{3,2},{4,5},{5,4},{6,7},{7,6},{8,9},{9,8},{10,11... | collective-permute-start | bytes 22020104 | tf_op jit(solution)/shard_map/ppermute | solution.py:112
  171.5 18.7 %copy-start.4 = (f32[64,28,16]{0,2,1:T(8,128)S(1)}, f32[64,28,16]{0,2,1:T(8,128)}, u32[]{:S(2)}) copy-start(f32[64,28,16]{0,2,1:T(8,128)} %param.15) | copy-start | bytes 344068
  171.5 125.0 %all-to-all-start.2 = ((bf16[64,16,3584]{2,1,0:T(8,128)(2,1)}), bf16[64,16,3584]{2,1,0:T(8,128)(2,1)}, u32[]{:S(2)}, u32[]{:S(2)}) async-start(bf16[64,16,3584]{2,1,0:T(8,128)(2,1)} %bitcast.50), calls=%async_computation.2 | async-start | bytes 14680064 | tf_op jit(solution)/shard_map/all_to_all | solution.py:100
  189.7 7.0 %collective-permute-start.1 = (bf16[64,8,3584]{2,1,0:T(8,128)(2,1)}, bf16[64,8,3584]{2,1,0:T(8,128)(2,1)}, u32[]{:S(2)}, u32[]{:S(2)}) collective-permute-start(bf16[64,8,3584]{2,1,0:T(8,128)(2,1)} %all-to-all-done.own_ref), channel_id=1, source_target_pairs={{0,1},{1,0},{2,3},{3,2},{4,5},{5,4},{6,7},{7,6},{8,9},{9,8},{10,11... | collective-permute-start | bytes 11010056 | tf_op jit(solution)/shard_map/ppermute | solution.py:103
  190.3 2.8 copy-start.5
  206.9 2.9 copy-start.2
  296.5 71.3 %all-to-all-start.3 = ((bf16[64,4,3584]{2,1,0:T(4,128)(2,1)}), bf16[64,4,3584]{2,1,0:T(4,128)(2,1)S(1)}, u32[]{:S(2)}, u32[]{:S(2)}) async-start(bf16[64,4,3584]{2,1,0:T(4,128)(2,1)} %reshape.62), calls=%async_computation.3 | async-start | bytes 3670016 | tf_op jit(solution)/shard_map/all_to_all | solution.py:100
  312.2 45.7 %slice-start = ((s8[7340032]{0:T(1024)(128)(4,1)}), s8[3145728]{0:T(1024)(128)(4,1)S(1)}, s32[]{:S(2)}) async-start(s8[7340032]{0:T(1024)(128)(4,1)} %bitcast.45), calls=%async_computation.6 | async-start | bytes 6291456
  337.7 20.2 %slice-start.1 = ((s8[7340032]{0:T(1024)(128)(4,1)}), s8[4194304]{0:T(1024)(128)(4,1)S(1)}, s32[]{:S(2)}) async-start(s8[7340032]{0:T(1024)(128)(4,1)} %bitcast.45), calls=%async_computation.7 | async-start | bytes 8388608
  367.8 1.3 copy-start.3
  369.1 107.2 %all-to-all-start.4 = ((bf16[64,16,3584]{2,1,0:T(8,128)(2,1)}), bf16[64,16,3584]{2,1,0:T(8,128)(2,1)}, u32[]{:S(2)}, u32[]{:S(2)}) async-start(bf16[64,16,3584]{2,1,0:T(8,128)(2,1)} %bitcast.51), calls=%async_computation.4 | async-start | bytes 14680064 | tf_op jit(solution)/shard_map/all_to_all | solution.py:100
  379.7 12.1 %slice-start.2 = ((s8[7340032]{0:T(1024)(128)(4,1)}), s8[3145728]{0:T(1024)(128)(4,1)S(1)}, s32[]{:S(2)}) async-start(s8[7340032]{0:T(1024)(128)(4,1)} %bitcast.47), calls=%async_computation.8 | async-start | bytes 6291456
  383.8 7.9 %slice-start.3 = ((s8[7340032]{0:T(1024)(128)(4,1)}), s8[4194304]{0:T(1024)(128)(4,1)S(1)}, s32[]{:S(2)}) async-start(s8[7340032]{0:T(1024)(128)(4,1)} %bitcast.47), calls=%async_computation.9 | async-start | bytes 8388608
  395.1 98.1 %copy-start.7 = (bf16[128,8]{0,1:T(8,128)(2,1)S(1)}, bf16[128,8]{0,1:T(8,128)(2,1)}, u32[]{:S(2)}) copy-start(bf16[128,8]{0,1:T(8,128)(2,1)} %param.12) | copy-start | bytes 6148
  395.1 98.1 %copy-start.9 = (bf16[128,3584]{1,0:T(8,128)(2,1)S(1)}, bf16[128,3584]{1,0:T(8,128)(2,1)}, u32[]{:S(2)}) copy-start(bf16[128,3584]{1,0:T(8,128)(2,1)} %param.10) | copy-start | bytes 2752516
  476.3 40.2 %all-to-all-start.5 = ((bf16[64,4,3584]{2,1,0:T(4,128)(2,1)}), bf16[64,4,3584]{2,1,0:T(4,128)(2,1)S(1)}, u32[]{:S(2)}, u32[]{:S(2)}) async-start(bf16[64,4,3584]{2,1,0:T(4,128)(2,1)} %reshape.70), calls=%async_computation.5 | async-start | bytes 3670016 | tf_op jit(solution)/shard_map/all_to_all | solution.py:100
  517.8 5.8 %copy-start.1 = (bf16[128,3584]{1,0:T(8,128)(2,1)S(1)}, bf16[128,3584]{1,0:T(8,128)(2,1)}, u32[]{:S(2)}) copy-start(bf16[128,3584]{1,0:T(8,128)(2,1)} %param.9) | copy-start | bytes 2752516

commit v2 on v1

--- a/solution.py
+++ b/solution.py
@@ -7,8 +7,12 @@
 
 FF = 1024
 TOP = 8
-MOST = 20
-FIRST = 16
+PEERS = 16
+COLS = 256
+
+
+def in_rows(block):
+    return block.astype(jnp.float32).reshape(-1, block.shape[-1]).astype(jnp.bfloat16)
 
 
 def gu_kernel(parity_ref, own_ref, other_ref, scale_ref, out_ref):
@@ -33,8 +37,9 @@
 
 
 def dequantize_gu(own, other, scales, parity):
-    chips, _, packed = own.shape
-    width = packed * 2 // 7
+    chips = own.shape[0]
+    width = 2 * FF
+    packed = width * 7 // 2
     return pl.pallas_call(
         gu_kernel,
         grid=(chips // 2,),
@@ -66,14 +71,15 @@
 
 
 def dequantize_down(own, other, scales, parity):
-    chips, _, width = own.shape
+    chips = own.shape[0]
+    width = scales.shape[1]
     return pl.pallas_call(
         down_kernel,
         grid=(chips // 4,),
         in_specs=[
             pl.BlockSpec(memory_space=pltpu.SMEM),
-            pl.BlockSpec((4, 8, width), lambda i: (i, 0, 0)),
-            pl.BlockSpec((4, 8, width), lambda i: (i, 0, 0)),
+            pl.BlockSpec((4, 8, width), lambda i: (i, 0, 2)),
+            pl.BlockSpec((4, 8, width), lambda i: (i, 0, 2)),
             pl.BlockSpec(scales.shape, lambda i: (0, 0)),
         ],
         out_specs=pl.BlockSpec((64, width), lambda i: (i, 0)),
@@ -84,10 +90,187 @@
     )(parity, own, other, scales)
 
 
+def expert_kernel(x_ref, gu_hbm, down_hbm, out_ref, gu_ref, down_ref, rows_ref, active_ref, sems):
+    step = pl.program_id(0)
+    width = rows_ref.shape[1]
+    half = width // 2
+    eight = 8 * PEERS
+    chunks = FF // COLS
+    copies = []
+    for j in range(chunks):
+        for start in (j * COLS, FF + j * COLS):
+            part = (slice(None), pl.ds(start, COLS))
+            copies.append(
+                pltpu.make_async_copy(gu_hbm.at[part], gu_ref.at[part], sems.at[len(copies)])
+            )
+    copies.append(pltpu.make_async_copy(down_hbm, down_ref, sems.at[len(copies)]))
+
+    @pl.when(step == 0)
+    def _():
+        for copy in copies:
+            copy.start()
+
+    for q in range(0, PEERS, 4):
+        for g in range(2):
+            rows_ref[pl.ds(g * eight + 8 * q, 32), :] = in_rows(
+                x_ref[q : q + 4, :, g * width : (g + 1) * width]
+            )
+        fold = [x_ref[p, :, 2 * width :].astype(jnp.float32) for p in range(q, q + 4)]
+        for part, first in ((0, 0), (1, 4)):
+            rows_ref[pl.ds(2 * eight + 4 * q, 16), pl.ds(part * half, half)] = jnp.concatenate(
+                [f[first : first + 4] for f in fold], axis=0
+            ).astype(jnp.bfloat16)
+
+    for j in range(chunks):
+
+        @pl.when(step == 0)
+        def _():
+            copies[2 * j].wait()
+            copies[2 * j + 1].wait()
+
+        gate = jnp.dot(
+            rows_ref[...], gu_ref[:, j * COLS : (j + 1) * COLS], preferred_element_type=jnp.float32
+        )
+        up = jnp.dot(
+            rows_ref[...],
+            gu_ref[:, FF + j * COLS : FF + (j + 1) * COLS],
+            preferred_element_type=jnp.float32,
+        )
+        active_ref[:, j * COLS : (j + 1) * COLS] = (gate / (1.0 + jnp.exp(-gate)) * up).astype(
+            jnp.bfloat16
+        )
+
+    @pl.when(step == 0)
+    def _():
+        copies[-1].wait()
+
+    for j in range(half // COLS):
+        sides = []
+        for side in range(2):
+            at = side * half + j * COLS
+            y = jnp.dot(
+                active_ref[...], down_ref[:, at : at + COLS], preferred_element_type=jnp.float32
+            )
+            sides.append(y)
+            for g in range(2):
+                out_ref[:, :, g * width + at : g * width + at + COLS] = (
+                    y[g * eight : (g + 1) * eight].reshape(PEERS, 8, COLS).astype(jnp.bfloat16)
+                )
+        for p in range(PEERS):
+            at = 2 * eight + 4 * p
+            out_ref[p, :, 2 * width + j * COLS : 2 * width + (j + 1) * COLS] = jnp.concatenate(
+                [sides[0][at : at + 4], sides[1][at : at + 4]], axis=0
+            ).astype(jnp.bfloat16)
+
+
+def run_expert(arrived, w_gu, w_down):
+    peers, _, packed = arrived.shape
+    width = w_gu.shape[0]
+    rows = peers * 20
+    return pl.pallas_call(
+        expert_kernel,
+        grid=(peers // PEERS,),
+        in_specs=[
+            pl.BlockSpec((PEERS, 8, packed), lambda i: (i, 0, 0)),
+            pl.BlockSpec(memory_space=pl.ANY),
+            pl.BlockSpec(memory_space=pl.ANY),
+        ],
+        out_specs=pl.BlockSpec((PEERS, 8, packed), lambda i: (i, 0, 0)),
+        out_shape=jax.ShapeDtypeStruct(arrived.shape, jnp.bfloat16),
+        scratch_shapes=[
+            pltpu.VMEM(w_gu.shape, jnp.bfloat16),
+            pltpu.VMEM(w_down.shape, jnp.bfloat16),
+            pltpu.VMEM((PEERS * 20, width), jnp.bfloat16),
+            pltpu.VMEM((PEERS * 20, FF), jnp.bfloat16),
+            pltpu.SemaphoreType.DMA((2 * FF // COLS + 1,)),
+        ],
+        compiler_params=pltpu.CompilerParams(vmem_limit_bytes=56 * 1024 * 1024),
+        cost_estimate=pl.CostEstimate(
+            flops=rows * width * FF * 6,
+            bytes_accessed=rows * width * 4 + width * FF * 6,
+            transcendentals=rows * FF,
+        ),
+        name="run_expert",
+    )(arrived, w_gu, w_down)
+
+
+def combine_kernel(x_ref, rank_ref, gate_ref, cotangent_ref, out_ref, grad_ref, sum_ref):
+    step = pl.program_id(0)
+    tokens, width = cotangent_ref.shape
+    half = width // 2
+
+    @pl.when(step == 0)
+    def _():
+        sum_ref[...] = jnp.zeros_like(sum_ref)
+
+    rank = rank_ref[...][:, None, :]
+    gate = gate_ref[...][:, None, :]
+    shape = (PEERS, 8, tokens)
+    row = lax.broadcasted_iota(jnp.int32, shape, 1)
+    low = row < 4
+    pieces = [
+        (rank == row, 0, 0, width),
+        (rank == row + 8, width, 0, width),
+        ((rank == row + 16) & low, 2 * width, 0, half),
+        ((rank == row + 12) & ~low, 2 * width, half, half),
+    ]
+    grad = jnp.zeros((PEERS, tokens), jnp.float32)
+    for mask, source, place, count in pieces:
+        rows = in_rows(x_ref[:, :, source : source + count])
+        weight = jnp.where(mask, gate, 0.0).reshape(-1, tokens).astype(jnp.bfloat16)
+        sum_ref[:, place : place + count] += lax.dot_general(
+            weight, rows, (((0,), (0,)), ((), ())), preferred_element_type=jnp.float32
+        )
+        inner = lax.dot_general(
+            rows,
+            cotangent_ref[:, place : place + count],
+            (((1,), (1,)), ((), ())),
+            preferred_element_type=jnp.float32,
+        )
+        grad += jnp.sum(jnp.where(mask, inner.reshape(shape), 0.0), axis=1)
+    grad_ref[...] = grad
+
+    @pl.when(step == pl.num_programs(0) - 1)
+    def _():
+        out_ref[...] = sum_ref[...].astype(jnp.bfloat16)
+
+
+def combine(returned, rank, gate_of, cotangent):
+    peers, _, packed = returned.shape
+    tokens, width = cotangent.shape
+    return pl.pallas_call(
+        combine_kernel,
+        grid=(peers // PEERS,),
+        in_specs=[
+            pl.BlockSpec((PEERS, 8, packed), lambda i: (i, 0, 0)),
+            pl.BlockSpec((PEERS, tokens), lambda i: (i, 0)),
+            pl.BlockSpec((PEERS, tokens), lambda i: (i, 0)),
+            pl.BlockSpec((tokens, width), lambda i: (0, 0)),
+        ],
+        out_specs=[
+            pl.BlockSpec((tokens, width), lambda i: (0, 0)),
+            pl.BlockSpec((PEERS, tokens), lambda i: (i, 0)),
+        ],
+        out_shape=[
+            jax.ShapeDtypeStruct((tokens, width), jnp.bfloat16),
+            jax.ShapeDtypeStruct((peers, tokens), jnp.float32),
+        ],
+        scratch_shapes=[pltpu.VMEM((tokens, width), jnp.float32)],
+        compiler_params=pltpu.CompilerParams(vmem_limit_bytes=40 * 1024 * 1024),
+        cost_estimate=pl.CostEstimate(
+            flops=peers * 24 * tokens * width * 4,
+            bytes_accessed=peers * 40 * width + tokens * width * 4,
+            transcendentals=0,
+        ),
+        name="combine",
+    )(returned, rank, gate_of, cotangent)
+
+
 def shards(
     tokens, cotangent, routes, gates, previous_row, gu_payload, gu_scales, down_payload, down_scales
 ):
     local_count, model_width = tokens.shape
+    half = model_width // 2
     devices = lax.axis_size("expert")
     experts = previous_row.shape[0]
     device_id = lax.axis_index("expert")
@@ -99,17 +282,14 @@
     def exchange(x):
         return lax.all_to_all(x, "expert", 0, 0, axis_index_groups=same_core, tiled=True)
 
-    down_own = exchange(down_payload)
-    down_other = lax.ppermute(down_own, "expert", swap)
-
-    packed_gu = jnp.concatenate(
+    packed = jnp.concatenate(
         [gu_payload[:, 8 * g : 8 * g + 8] for g in range(3)]
-        + [jnp.concatenate([gu_payload[:, 24:28, :FF], gu_payload[:, 24:28, FF:]], axis=1)],
+        + [jnp.concatenate([gu_payload[:, 24:28, :FF], gu_payload[:, 24:28, FF:]], axis=1)]
+        + [down_payload],
         axis=2,
     )
-    packed_gu, down_own = lax.optimization_barrier((packed_gu, down_own))
-    gu_own = exchange(packed_gu)
-    gu_other = lax.ppermute(gu_own, "expert", swap)
+    tokens, packed = lax.optimization_barrier((tokens, packed))
+    own = exchange(packed)
 
     routes_t = routes.T
     gates_t = gates.T.astype(jnp.float32)
@@ -126,57 +306,27 @@
     ).astype(jnp.int32)
     rank = jnp.where(member, rank, -1)
 
-    w_down = dequantize_down(
-        down_own, down_other, jnp.repeat(down_scales[chip], 128, axis=1), parity
-    )
-    w_gu = dequantize_gu(gu_own, gu_other, jnp.repeat(gu_scales[chip], 128, axis=1), parity)
-
-    def chosen(start, count):
-        places = jnp.arange(start, start + count, dtype=jnp.int32)[None, :, None]
-        return rank[:, None, :] == places
-
-    def dispatch(start, count, after):
-        select = chosen(start, count).reshape(experts * count, local_count).astype(jnp.bfloat16)
-        outgoing = jnp.dot(select, tokens, preferred_element_type=jnp.float32).astype(jnp.bfloat16)
-        outgoing = outgoing.reshape(experts, count, model_width)
-        outgoing, after = lax.optimization_barrier((outgoing, after))
-        return exchange(outgoing), after
-
-    def expert(arrived):
-        rows = arrived.reshape(-1, model_width)
-        hidden = jnp.dot(rows, w_gu, preferred_element_type=jnp.float32)
-        active = (jax.nn.silu(hidden[:, :FF]) * hidden[:, FF:]).astype(jnp.bfloat16)
-        result = jnp.dot(active, w_down, preferred_element_type=jnp.float32).astype(jnp.bfloat16)
-        return result.reshape(arrived.shape)
-
-    def combine(returned, start, count):
-        mask = chosen(start, count)
-        rows = returned.reshape(-1, model_width)
-        weight = jnp.where(mask, gate_of[:, None, :], 0.0).astype(jnp.bfloat16)
-        summed = lax.dot_general(
-            weight.reshape(-1, local_count),
-            rows,
-            (((0,), (0,)), ((), ())),
-            preferred_element_type=jnp.float32,
-        )
-        inner = lax.dot_general(
-            rows, cotangent, (((1,), (1,)), ((), ())), preferred_element_type=jnp.float32
-        ).reshape(mask.shape)
-        return summed, jnp.sum(jnp.where(mask, inner, 0.0), axis=1)
-
-    rest = MOST - FIRST
-    arrived_a, gu_own = dispatch(0, FIRST, gu_own)
-    arrived_b, arrived_a = dispatch(FIRST, rest, arrived_a)
-    produced_a = expert(arrived_a)
-    produced_a, arrived_b = lax.optimization_barrier((produced_a, arrived_b))
-    returned_a = exchange(produced_a)
-    produced_b = expert(arrived_b)
-    produced_b, returned_a = lax.optimization_barrier((produced_b, returned_a))
-    returned_b = exchange(produced_b)
-    out_a, grad_a = combine(returned_a, 0, FIRST)
-    out_b, grad_b = combine(returned_b, FIRST, rest)
-    layer_out = (out_a + out_b).astype(jnp.bfloat16)
-    grad = grad_a + grad_b
+    def picked(places):
+        select = (rank[:, None, :] == places[None, :, None]).astype(jnp.bfloat16)
+        rows = jnp.dot(
+            select.reshape(-1, local_count), tokens, preferred_element_type=jnp.float32
+        ).astype(jnp.bfloat16)
+        return rows.reshape(experts, places.shape[0], model_width)
+
+    eight = jnp.arange(8, dtype=jnp.int32)
+    last = picked(16 + eight % 4)
+    last = jnp.where(eight[None, :, None] < 4, last[:, :, :half], last[:, :, half:])
+    outgoing = jnp.concatenate([picked(eight), picked(8 + eight), last], axis=2)
+
+    outgoing, own = lax.optimization_barrier((outgoing, own))
+    other = lax.ppermute(own, "expert", swap)
+    arrived = exchange(outgoing)
+    w_down = dequantize_down(own, other, jnp.repeat(down_scales[chip], 128, axis=1), parity)
+    w_gu = dequantize_gu(own, other, jnp.repeat(gu_scales[chip], 128, axis=1), parity)
+    w_gu, w_down, arrived = lax.optimization_barrier((w_gu, w_down, arrived))
+    produced = run_expert(arrived, w_gu, w_down)
+    returned = exchange(produced)
+    layer_out, grad = combine(returned, rank, gate_of, cotangent)
     gate_grad = jnp.sum(jnp.where(named, grad[None], 0.0), axis=1).T
     return (layer_out, gate_grad)
 

time: 525 us -> 565 us (1.076)
  waiting for transfers between devices: 313 us -> 384 us
  matrix products: 58.7 us -> 3.61 us
  Pallas kernels: 35.6 us -> 83 us
  starting transfers between devices: 85.9 us -> 60.5 us
    all_to_all x6 -> x3, waiting for transfers between devices: 309 us -> 384 us  [exchange(): lax.all_to_all(x, 'expert', 0, 0, axis_index_groups=same_core, tiled=True)]
    dot_general x10 -> x3, matrix products: 58.6 us -> 3.47 us  [picked(): jnp.dot(select.reshape(-1, local_count), tokens, preferred_element_type=j...]
    pallas_call x0 -> x2, Pallas kernels: none -> 47.5 us  [the longest x1 38.2 us: run_expert(): pl.pallas_call(expert_kernel, grid=(peers // PEERS,), in_specs=[pl.BlockS...]
    all_to_all x6 -> x3, starting transfers between devices: 85.4 us -> 60.5 us  [exchange(): lax.all_to_all(x, 'expert', 0, 0, axis_index_groups=same_core, tiled=True)]
    reshape x3 -> x0, local copies, waits for them, and re-layouts: 9.72 us -> none  [the longest x1 4.16 us: expert(): return result.reshape(arrived.shape)]
    unnamed x35 -> x27, local copies, waits for them, and re-layouts: 8.63 us -> 11.4 us
  transfers between devices with their start and end apart: 8 -> 4, of which waited for: 6 -> 3; matrix products, arithmetic and copies ran while one was open for 15% -> 2% of each run, Pallas kernels for 7% -> 6%
where the time goes in v2:
time: 565 us; the launch traced here: 559 us
  waiting for transfers between devices  384 us (68%)
  Pallas kernels  83 us (15%)
  starting transfers between devices  60.5 us (11%)
  local copies, waits for them, and re-layouts  20.1 us (4%)
  other arithmetic  6.48 us (1%)
    all_to_all x3, waiting for transfers between devices, exchange(): lax.all_to_all(x, 'expert', 0, 0, axis_index_groups=same_core, tiled=True)  384 us
    all_to_all x3, starting transfers between devices, exchange(): lax.all_to_all(x, 'expert', 0, 0, axis_index_groups=same_core, tiled=True)  60.5 us
    pallas_call x1, Pallas kernels, run_expert(): pl.pallas_call(expert_kernel, grid=(peers // PEERS,), in_specs=[pl.BlockS...  38.2 us
    pallas_call x1, Pallas kernels, dequantize_gu(): pl.pallas_call(gu_kernel, grid=(chips // 2,), in_specs=[pl.BlockSpec(memo...  25.3 us
    unnamed x27, local copies, waits for them, and re-layouts  11.4 us
  transfers between devices with their start and end apart: 4, of which 3 were waited for; matrix products, arithmetic and copies ran while one was open for 2% of the time, Pallas kernels for 6%

profile of v2, /device:TPU:0, one launch (start us, length us, event | category | flops | bytes accessed | tf_op | source)
XLA Modules:
  0.0 558.7 jit_solution(14284736422432652891)
XLA Ops:
  0.6 0.0 copy-start
  0.6 4.0 fusion.13
  4.7 1.3 fusion.12
  6.0 2.5 copy_dynamic-update-slice_fusion.2
  8.5 0.0 copy-start.4
  8.5 0.4 copy.38
  8.9 0.4 copy.37
  9.3 2.5 copy_dynamic-update-slice_fusion.1
  11.9 2.5 copy_dynamic-update-slice_fusion
  14.4 1.6 maximum_dynamic-update-slice_fusion
  16.0 0.0 copy-done.4
  16.0 2.1 constant_dynamic-update-slice_fusion
  18.1 0.0 copy-start.7
  18.1 0.0 copy-start.9
  18.1 11.9 %all-to-all-start = ((bf16[64,8,10752]{2,1,0:T(8,128)(2,1)}), bf16[64,8,10752]{2,1,0:T(8,128)(2,1)}, u32[]{:S(2)}, u32[]{:S(2)}) async-start(bf16[64,8,10752]{2,1,0:T(8,128)(2,1)} %constant_dynamic-update-slice_fusion), calls=%async_computation | async-start | bytes 22020096 | tf_op jit(solution)/shard_map/all_to_all | solution.py:283
  30.0 0.1 eq.99
  30.1 0.1 eq.95
  30.2 0.1 eq.91
  30.3 0.0 copy-done.7
  30.3 0.0 copy-done.9
  30.3 0.1 select_reduce_fusion.2
  30.5 0.1 fusion.3.rank_ref
  30.6 0.0 copy-done
  30.6 1.2 fusion.2
  31.8 1.2 fusion.1
  33.0 1.2 fusion
  34.1 0.2 slice_select_fusion
  34.4 3.8 pad_maximum_fusion
  38.2 0.0 copy-start.5
  38.2 0.0 copy-start.6
  38.2 156.3 %all-to-all-done.own_ref = bf16[64,8,10752]{2,1,0:T(8,128)(2,1)} async-done(((bf16[64,8,10752]{2,1,0:T(8,128)(2,1)}), bf16[64,8,10752]{2,1,0:T(8,128)(2,1)}, u32[]{:S(2)}, u32[]{:S(2)}) %all-to-all-start) | async-done | bytes 11010080 | tf_op jit(solution)/shard_map/all_to_all | solution.py:283
  194.4 0.0 collective-permute-start
  194.4 19.1 %all-to-all-start.1 = ((bf16[64,8,8960]{2,1,0:T(8,128)(2,1)}), bf16[64,8,8960]{2,1,0:T(8,128)(2,1)}, u32[]{:S(2)}, u32[]{:S(2)}) async-start(bf16[64,8,8960]{2,1,0:T(8,128)(2,1)} %pad_maximum_fusion), calls=%async_computation.1 | async-start | bytes 18350080 | tf_op jit(solution)/shard_map/all_to_all | solution.py:283
  213.6 0.0 copy-done.5
  213.6 0.1 constant_dynamic-slice_fusion
  213.7 0.2 copy.41
  214.0 0.1 broadcast_in_dim.71
  214.1 0.1 copy.43
  214.2 0.0 copy-done.6
  214.2 0.1 constant_dynamic-slice_fusion.1
  214.3 0.2 copy.42
  214.6 0.1 broadcast_bitcast_fusion.scale_ref
  214.7 0.0 collective-permute-done.other_ref
  214.7 10.2 %dequantize_down.1.down_hbm = bf16[1024,3584]{1,0:T(8,128)(2,1)S(1)} custom-call(s32[1]{0:T(128)} %bitcast.parity_ref, bf16[64,8,10752]{2,1,0:T(8,128)(2,1)} %all-to-all-done.own_ref, bf16[64,8,10752]{2,1,0:T(8,128)(2,1)} %collective-permute-done.other_ref, f32[8,3584]{1,0:T(8,128)S(1)} %broadcast_bitcast_fusion.scale_ref), custom_call_target="tpu_custom_call" | custom-call | flops 3670016 | bytes 14680064 | tf_op jit(solution)/shard_map/dequantize_down/pallas_call | solution.py:76
  224.9 0.0 copy-start.2
  224.9 2.9 copy-done.2
  227.8 25.3 %dequantize_gu.1.gu_hbm = bf16[3584,2048]{1,0:T(8,128)(2,1)} custom-call(s32[1]{0:T(128)} %bitcast.parity_ref, bf16[64,8,10752]{2,1,0:T(8,128)(2,1)} %all-to-all-done.own_ref, bf16[64,8,10752]{2,1,0:T(8,128)(2,1)} %collective-permute-done.other_ref, f32[28,2048]{1,0:T(8,128)S(1)} %bitcast.31), custom_call_target="tpu_custom_call" | custom-call | flops 7340032 | bytes 29360128 | tf_op jit(solution)/shard_map/dequantize_gu/pallas_call | solution.py:43
  253.1 91.6 %all-to-all-done.1.x_ref = bf16[64,8,8960]{2,1,0:T(8,128)(2,1)} async-done(((bf16[64,8,8960]{2,1,0:T(8,128)(2,1)}), bf16[64,8,8960]{2,1,0:T(8,128)(2,1)}, u32[]{:S(2)}, u32[]{:S(2)}) %all-to-all-start.1) | async-done | bytes 9175072 | tf_op jit(solution)/shard_map/all_to_all | solution.py:283
  344.7 38.2 %run_expert.1 = bf16[64,8,8960]{2,1,0:T(8,128)(2,1)} custom-call(bf16[64,8,8960]{2,1,0:T(8,128)(2,1)} %all-to-all-done.1.x_ref, bf16[3584,2048]{1,0:T(8,128)(2,1)} %dequantize_gu.1.gu_hbm, bf16[1024,3584]{1,0:T(8,128)(2,1)} %copy-done.2), custom_call_target="tpu_custom_call" | custom-call | flops 28185722880 | bytes 40370176 | tf_op jit(solution)/shard_map/run_expert/pallas_call | solution.py:170
  382.9 0.0 copy-start.8
  382.9 0.0 copy-start.3
  382.9 29.5 %all-to-all-start.2 = ((bf16[64,8,8960]{2,1,0:T(8,128)(2,1)}), bf16[64,8,8960]{2,1,0:T(8,128)(2,1)}, u32[]{:S(2)}, u32[]{:S(2)}) async-start(bf16[64,8,8960]{2,1,0:T(8,128)(2,1)} %run_expert.1), calls=%async_computation.2 | async-start | bytes 18350080 | tf_op jit(solution)/shard_map/all_to_all | solution.py:283
  412.5 0.0 copy-done.8
  412.5 0.0 copy-start.1
  412.6 136.2 %all-to-all-done.2.x_ref = bf16[64,8,8960]{2,1,0:T(8,128)(2,1)} async-done(((bf16[64,8,8960]{2,1,0:T(8,128)(2,1)}), bf16[64,8,8960]{2,1,0:T(8,128)(2,1)}, u32[]{:S(2)}, u32[]{:S(2)}) %all-to-all-start.2) | async-done | bytes 9175072 | tf_op jit(solution)/shard_map/all_to_all | solution.py:283
  548.8 0.0 copy-done.3
  548.8 9.3 %combine.1 = (bf16[128,3584]{1,0:T(8,128)(2,1)}, f32[64,128]{1,0:T(8,128)S(1)}) custom-call(bf16[64,8,8960]{2,1,0:T(8,128)(2,1)} %all-to-all-done.2.x_ref, s32[64,128]{1,0:T(8,128)S(1)} %fusion.3.rank_ref, f32[64,128]{1,0:T(8,128)S(1)} %select_reduce_fusion.1.gate_ref, bf16[128,3584]{1,0:T(8,128)(2,1)S(1)} %copy-done.3), custom_call_target="tpu_custom_call" | custom-call | flops 2818572288 | bytes 11010048 | tf_op jit(solution)/shard_map/combine/pallas_call | solution.py:241
  558.1 0.6 select_reduce_fusion
  558.7 0.0 copy-done.1
  (10 shorter events, 0.1 us)
Async XLA Ops:
  0.6 30.0 %copy-start = (bf16[128,3584]{1,0:T(8,128)(2,1)S(1)}, bf16[128,3584]{1,0:T(8,128)(2,1)}, u32[]{:S(2)}) copy-start(bf16[128,3584]{1,0:T(8,128)(2,1)} %param.9) | copy-start | bytes 2752516
  8.5 7.5 %copy-start.4 = (bf16[64,8,3584]{2,1,0:T(8,128)(2,1)S(1)}, bf16[64,8,3584]{2,1,0:T(8,128)(2,1)}, u32[]{:S(2)}) copy-start(bf16[64,8,3584]{2,1,0:T(8,128)(2,1)} %param.16) | copy-start | bytes 11010052
  18.1 12.2 %copy-start.7 = (s32[128,8]{0,1:T(8,128)S(1)}, s32[128,8]{0,1:T(8,128)}, u32[]{:S(2)}) copy-start(s32[128,8]{0,1:T(8,128)} %param.11) | copy-start | bytes 12292
  18.1 12.2 %copy-start.9 = (s32[64]{0:T(128)S(1)}, s32[64]{0:T(128)}, u32[]{:S(2)}) copy-start(s32[64]{0:T(128)} %param.13) | copy-start | bytes 772
  18.1 176.3 %all-to-all-start = ((bf16[64,8,10752]{2,1,0:T(8,128)(2,1)}), bf16[64,8,10752]{2,1,0:T(8,128)(2,1)}, u32[]{:S(2)}, u32[]{:S(2)}) async-start(bf16[64,8,10752]{2,1,0:T(8,128)(2,1)} %constant_dynamic-update-slice_fusion), calls=%async_computation | async-start | bytes 22020096 | tf_op jit(solution)/shard_map/all_to_all | solution.py:283
  38.2 175.4 %copy-start.5 = (f32[64,28,16]{0,2,1:T(8,128)S(1)}, f32[64,28,16]{0,2,1:T(8,128)}, u32[]{:S(2)}) copy-start(f32[64,28,16]{0,2,1:T(8,128)} %param.15) | copy-start | bytes 344068
  38.2 176.1 %copy-start.6 = (f32[64,8,28]{0,1,2:T(8,128)S(1)}, f32[64,8,28]{0,1,2:T(8,128)}, u32[]{:S(2)}) copy-start(f32[64,8,28]{0,1,2:T(8,128)} %param.17) | copy-start | bytes 172036
  194.4 20.3 %collective-permute-start = (bf16[64,8,10752]{2,1,0:T(8,128)(2,1)}, bf16[64,8,10752]{2,1,0:T(8,128)(2,1)}, u32[]{:S(2)}, u32[]{:S(2)}) collective-permute-start(bf16[64,8,10752]{2,1,0:T(8,128)(2,1)} %all-to-all-done.own_ref), channel_id=1, source_target_pairs={{0,1},{1,0},{2,3},{3,2},{4,5},{5,4},{6,7},{7,6},{8,9},{9,8},{10,11... | collective-permute-start | bytes 33030152 | tf_op jit(solution)/shard_map/ppermute | solution.py:322
  194.4 150.3 %all-to-all-start.1 = ((bf16[64,8,8960]{2,1,0:T(8,128)(2,1)}), bf16[64,8,8960]{2,1,0:T(8,128)(2,1)}, u32[]{:S(2)}, u32[]{:S(2)}) async-start(bf16[64,8,8960]{2,1,0:T(8,128)(2,1)} %pad_maximum_fusion), calls=%async_computation.1 | async-start | bytes 18350080 | tf_op jit(solution)/shard_map/all_to_all | solution.py:283
  224.9 2.9 copy-start.2
  382.9 29.6 %copy-start.8 = (bf16[128,8]{0,1:T(8,128)(2,1)S(1)}, bf16[128,8]{0,1:T(8,128)(2,1)}, u32[]{:S(2)}) copy-start(bf16[128,8]{0,1:T(8,128)(2,1)} %param.12) | copy-start | bytes 6148
  382.9 165.9 %copy-start.3 = (bf16[128,3584]{1,0:T(8,128)(2,1)S(1)}, bf16[128,3584]{1,0:T(8,128)(2,1)}, u32[]{:S(2)}) copy-start(bf16[128,3584]{1,0:T(8,128)(2,1)} %cotangent_ref.1) | copy-start | bytes 2752516
  382.9 165.8 %all-to-all-start.2 = ((bf16[64,8,8960]{2,1,0:T(8,128)(2,1)}), bf16[64,8,8960]{2,1,0:T(8,128)(2,1)}, u32[]{:S(2)}, u32[]{:S(2)}) async-start(bf16[64,8,8960]{2,1,0:T(8,128)(2,1)} %run_expert.1), calls=%async_computation.2 | async-start | bytes 18350080 | tf_op jit(solution)/shard_map/all_to_all | solution.py:283
  412.5 146.2 %copy-start.1 = (bf16[128,3584]{1,0:T(8,128)(2,1)S(1)}, bf16[128,3584]{1,0:T(8,128)(2,1)}, u32[]{:S(2)}) copy-start(bf16[128,3584]{1,0:T(8,128)(2,1)} %param.9) | copy-start | bytes 2752516

commit v3 on v2

v3 whole, which is shorter than its diff:
```python
import functools

import jax
import jax.numpy as jnp
from jax import lax
from jax.experimental import pallas as pl
from jax.experimental.pallas import tpu as pltpu
from jax.sharding import PartitionSpec as P

FF = 1024
TOP = 8
COLS = 256
GROUP = 16


def in_rows(block):
    return block.astype(jnp.float32).reshape(-1, block.shape[-1]).astype(jnp.bfloat16)


def by_core(parity_ref, own_ref, other_ref, body):
    @pl.when(parity_ref[0] == 0)
    def _():
        body(own_ref, other_ref)

    @pl.when(parity_ref[0] != 0)
    def _():
        body(other_ref, own_ref)


def gu_kernel(parity_ref, own_ref, other_ref, scale_ref, out_ref):
    step = pl.program_id(0)
    width = out_ref.shape[1]

    def body(zero_ref, one_ref):
        tiles = []
        for chip in range(zero_ref.shape[0]):
            zero = [zero_ref[chip, :, g * width : (g + 1) * width] for g in range(3)]
            one = [one_ref[chip, :, g * width : (g + 1) * width] for g in range(3)]
            fold_zero = zero_ref[chip, :, 3 * width :].astype(jnp.float32)
            fold_one = one_ref[chip, :, 3 * width :].astype(jnp.float32)
            middle = jnp.concatenate(
                [
                    jnp.concatenate([fold_zero[:4], fold_one[:4]], axis=0),
                    jnp.concatenate([fold_zero[4:], fold_one[4:]], axis=0),
                ],
                axis=1,
            )
            tiles += zero + [middle] + one
        for pair in range(len(tiles) // 2):
            scaled = []
            for k in (2 * pair, 2 * pair + 1):
                at = (step * 8 * len(tiles) + 8 * k) // 128
                scaled.append(tiles[k].astype(jnp.float32) * scale_ref[pl.ds(at, 1), :])
            out_ref[16 * pair : 16 * pair + 16, :] = jnp.concatenate(scaled, axis=0).astype(
                jnp.bfloat16
            )

    by_core(parity_ref, own_ref, other_ref, body)


def dequantize_gu(own, other, scales, parity):
    chips, _, packed = own.shape
    width = 2 * FF
    return pl.pallas_call(
        gu_kernel,
        grid=(chips // 2,),
        in_specs=[
            pl.BlockSpec(memory_space=pltpu.SMEM),
            pl.BlockSpec((2, 8, packed), lambda i: (i, 0, 0)),
            pl.BlockSpec((2, 8, packed), lambda i: (i, 0, 0)),
            pl.BlockSpec(scales.shape, lambda i: (0, 0)),
        ],
        out_specs=pl.BlockSpec((112, width), lambda i: (i, 0)),
        out_shape=jax.ShapeDtypeStruct((chips * 56, width), jnp.bfloat16),
        compiler_params=pltpu.CompilerParams(vmem_limit_bytes=32 * 1024 * 1024),
        cost_estimate=pl.CostEstimate(
            flops=chips * 56 * width, bytes_accessed=chips * 56 * width * 4, transcendentals=0
        ),
        name="dequantize_gu",
    )(parity, own, other, scales)


def down_kernel(parity_ref, own_ref, other_ref, scale_ref, out_ref):
    step = pl.program_id(0)
    chips = own_ref.shape[0]
    scale = scale_ref[pl.ds(step * chips * 16 // 128, 1), :]

    def body(zero_ref, one_ref):
        for chip in range(chips):
            both = [ref[chip].astype(jnp.float32) * scale for ref in (zero_ref, one_ref)]
            out_ref[16 * chip : 16 * chip + 16, :] = jnp.concatenate(both, axis=0).astype(
                jnp.bfloat16
            )

    by_core(parity_ref, own_ref, other_ref, body)


def dequantize_down(own, other, scales, parity):
    chips, _, width = own.shape
    return pl.pallas_call(
        down_kernel,
        grid=(chips // 8,),
        in_specs=[
            pl.BlockSpec(memory_space=pltpu.SMEM),
            pl.BlockSpec((8, 8, width), lambda i: (i, 0, 0)),
            pl.BlockSpec((8, 8, width), lambda i: (i, 0, 0)),
            pl.BlockSpec(scales.shape, lambda i: (0, 0)),
        ],
        out_specs=pl.BlockSpec((128, width), lambda i: (i, 0)),
        out_shape=jax.ShapeDtypeStruct((chips * 16, width), jnp.bfloat16),
        compiler_params=pltpu.CompilerParams(vmem_limit_bytes=32 * 1024 * 1024),
        cost_estimate=pl.CostEstimate(
            flops=chips * 16 * width, bytes_accessed=chips * 16 * width * 4, transcendentals=0
        ),
        name="dequantize_down",
    )(parity, own, other, scales)


def expert_kernel(place, x_ref, gu_hbm, down_hbm, *refs):
    out_ref, gu_ref, down_ref, rows_ref, active_ref, sems = refs[-6:]
    step = pl.program_id(0)
    peers, _, packed = x_ref.shape
    width = rows_ref.shape[1]
    half = width // 2
    full = packed // width
    eight = 8 * peers
    chunks = FF // COLS
    copies = []
    for j in range(chunks):
        for start in (j * COLS, FF + j * COLS):
            part = (slice(None), pl.ds(start, COLS))
            copies.append(
                pltpu.make_async_copy(gu_hbm.at[part], gu_ref.at[part], sems.at[len(copies)])
            )
    copies.append(pltpu.make_async_copy(down_hbm, down_ref, sems.at[len(copies)]))

    @pl.when(step == 0)
    def _():
        for copy in copies:
            copy.start()

    for q in range(0, peers, 4):
        for g in range(full):
            rows_ref[pl.ds(g * eight + 8 * q, 32), :] = in_rows(
                x_ref[q : q + 4, :, g * width : (g + 1) * width]
            )
        if packed > full * width:
            fold = [x_ref[p, :, full * width :].astype(jnp.float32) for p in range(q, q + 4)]
            for part, first in ((0, 0), (1, 4)):
                rows_ref[pl.ds(full * eight + 4 * q, 16), pl.ds(part * half, half)] = (
                    jnp.concatenate([f[first : first + 4] for f in fold], axis=0)
                ).astype(jnp.bfloat16)

    for j in range(chunks):

        @pl.when(step == 0)
        def _():
            copies[2 * j].wait()
            copies[2 * j + 1].wait()

        gate = jnp.dot(
            rows_ref[...], gu_ref[:, j * COLS : (j + 1) * COLS], preferred_element_type=jnp.float32
        )
        up = jnp.dot(
            rows_ref[...],
            gu_ref[:, FF + j * COLS : FF + (j + 1) * COLS],
            preferred_element_type=jnp.float32,
        )
        active_ref[:, j * COLS : (j + 1) * COLS] = (gate / (1.0 + jnp.exp(-gate)) * up).astype(
            jnp.bfloat16
        )

    @pl.when(step == 0)
    def _():
        copies[-1].wait()

    for j in range(half // COLS):
        sides = []
        for side in range(2):
            at = side * half + j * COLS
            y = jnp.dot(
                active_ref[...], down_ref[:, at : at + COLS], preferred_element_type=jnp.float32
            )
            sides.append(y)
            for g in range(full):
                to = place + g * width + at
                out_ref[:, :, to : to + COLS] = (
                    y[g * eight : (g + 1) * eight].reshape(peers, 8, COLS).astype(jnp.bfloat16)
                )
        if packed > full * width:
            for p in range(peers):
                at = full * eight + 4 * p
                to = place + full * width + j * COLS
                out_ref[p, :, to : to + COLS] = (
                    jnp.concatenate([sides[0][at : at + 4], sides[1][at : at + 4]], axis=0)
                ).astype(jnp.bfloat16)


def run_expert(arrived, w_gu, w_down, place, produced=None):
    peers, _, packed = arrived.shape
    width = w_gu.shape[0]
    each = 8 * packed // width
    group = 32
    rows = peers * each
    total = width * 5 // 2
    columns = total if produced is None else packed
    before = () if produced is None else (produced,)
    return pl.pallas_call(
        functools.partial(expert_kernel, place),
        grid=(peers // group,),
        in_specs=[
            pl.BlockSpec((group, 8, packed), lambda i: (i, 0, 0)),
            pl.BlockSpec(memory_space=pl.ANY),
            pl.BlockSpec(memory_space=pl.ANY),
        ]
        + [pl.BlockSpec(memory_space=pl.ANY)] * len(before),
        out_specs=pl.BlockSpec((group, 8, columns), lambda i: (i, 0, 0)),
        out_shape=jax.ShapeDtypeStruct((peers, 8, total), jnp.bfloat16),
        input_output_aliases={3: 0} if before else {},
        scratch_shapes=[
            pltpu.VMEM(w_gu.shape, jnp.bfloat16),
            pltpu.VMEM(w_down.shape, jnp.bfloat16),
            pltpu.VMEM((group * each, width), jnp.bfloat16),
            pltpu.VMEM((group * each, FF), jnp.bfloat16),
            pltpu.SemaphoreType.DMA((2 * FF // COLS + 1,)),
        ],
        compiler_params=pltpu.CompilerParams(vmem_limit_bytes=58 * 1024 * 1024),
        cost_estimate=pl.CostEstimate(
            flops=rows * width * FF * 6,
            bytes_accessed=rows * width * 4 + width * FF * 6,
            transcendentals=rows * FF,
        ),
        name="run_expert",
    )(arrived, w_gu, w_down, *before)


def combine_kernel(x_ref, rank_ref, gate_ref, cotangent_ref, out_ref, grad_ref, sum_ref):
    step = pl.program_id(0)
    tokens, width = cotangent_ref.shape
    half = width // 2

    @pl.when(step == 0)
    def _():
        sum_ref[...] = jnp.zeros_like(sum_ref)

    rank = rank_ref[...][:, None, :]
    gate = gate_ref[...][:, None, :]
    shape = (GROUP, 8, tokens)
    row = lax.broadcasted_iota(jnp.int32, shape, 1)
    low = row < 4
    pieces = [
        (rank == row, 0, 0, width),
        (rank == row + 8, width, 0, width),
        ((rank == row + 16) & low, 2 * width, 0, half),
        ((rank == row + 12) & ~low, 2 * width, half, half),
    ]
    grad = jnp.zeros((GROUP, tokens), jnp.float32)
    for mask, source, place, count in pieces:
        rows = in_rows(x_ref[:, :, source : source + count])
        weight = jnp.where(mask, gate, 0.0).reshape(-1, tokens).astype(jnp.bfloat16)
        sum_ref[:, place : place + count] += lax.dot_general(
            weight, rows, (((0,), (0,)), ((), ())), preferred_element_type=jnp.float32
        )
        inner = lax.dot_general(
            rows,
            cotangent_ref[:, place : place + count],
            (((1,), (1,)), ((), ())),
            preferred_element_type=jnp.float32,
        )
        grad += jnp.sum(jnp.where(mask, inner.reshape(shape), 0.0), axis=1)
    grad_ref[...] = grad

    @pl.when(step == pl.num_programs(0) - 1)
    def _():
        out_ref[...] = sum_ref[...].astype(jnp.bfloat16)


def combine(returned, rank, gate_of, cotangent):
    peers, _, packed = returned.shape
    tokens, width = cotangent.shape
    return pl.pallas_call(
        combine_kernel,
        grid=(peers // GROUP,),
        in_specs=[
            pl.BlockSpec((GROUP, 8, packed), lambda i: (i, 0, 0)),
            pl.BlockSpec((GROUP, tokens), lambda i: (i, 0)),
            pl.BlockSpec((GROUP, tokens), lambda i: (i, 0)),
            pl.BlockSpec((tokens, width), lambda i: (0, 0)),
        ],
        out_specs=[
            pl.BlockSpec((tokens, width), lambda i: (0, 0)),
            pl.BlockSpec((GROUP, tokens), lambda i: (i, 0)),
        ],
        out_shape=[
            jax.ShapeDtypeStruct((tokens, width), jnp.bfloat16),
            jax.ShapeDtypeStruct((peers, tokens), jnp.float32),
        ],
        scratch_shapes=[pltpu.VMEM((tokens, width), jnp.float32)],
        compiler_params=pltpu.CompilerParams(vmem_limit_bytes=40 * 1024 * 1024),
        cost_estimate=pl.CostEstimate(
            flops=peers * 24 * tokens * width * 4,
            bytes_accessed=peers * 40 * width + tokens * width * 4,
            transcendentals=0,
        ),
        name="combine",
    )(returned, rank, gate_of, cotangent)


def shards(
    tokens, cotangent, routes, gates, previous_row, gu_payload, gu_scales, down_payload, down_scales
):
    local_count, model_width = tokens.shape
    half = model_width // 2
    devices = lax.axis_size("expert")
    experts = previous_row.shape[0]
    device_id = lax.axis_index("expert")
    chip, core = device_id // 2, device_id % 2
    parity = core.astype(jnp.int32).reshape(1)
    same_core = [[2 * c + p for c in range(experts)] for p in range(2)]
    swap = [(d, d ^ 1) for d in range(devices)]

    def exchange(x):
        return lax.all_to_all(x, "expert", 0, 0, axis_index_groups=same_core, tiled=True)

    down_own = exchange(down_payload)
    packed = jnp.concatenate(
        [lax.dynamic_slice_in_dim(gu_payload, 4 * core + 8 * g, 8, axis=1) for g in range(3)]
        + [
            jnp.concatenate(
                [
                    lax.dynamic_slice_in_dim(gu_payload[:, :, half_ff : half_ff + FF], 24 - 24 * core, 4, axis=1)
                    for half_ff in (0, FF)
                ],
                axis=1,
            )
        ],
        axis=2,
    )
    gu_scale = jnp.repeat(gu_scales[chip], 128, axis=1)
    down_scale = jnp.repeat(down_scales[chip], 128, axis=1)

    routes_t = routes.T
    gates_t = gates.T.astype(jnp.float32)
    slots = jnp.arange(experts, dtype=jnp.int32)[None, :, None]
    target = jnp.sum(
        jnp.where(routes_t[:, None, :] == slots, previous_row[None, :, None], 0), axis=1
    )
    named = target[:, None, :] == slots
    member = jnp.any(named, axis=0)
    gate_of = jnp.sum(jnp.where(named, gates_t[:, None, :], 0.0), axis=0)
    earlier = jnp.arange(local_count)[:, None] < jnp.arange(local_count)[None, :]
    rank = jnp.dot(
        member.astype(jnp.bfloat16), earlier.astype(jnp.bfloat16), preferred_element_type=jnp.float32
    ).astype(jnp.int32)
    rank = jnp.where(member, rank, -1)

    def picked(places):
        select = (rank[:, None, :] == places[None, :, None]).astype(jnp.bfloat16)
        rows = jnp.dot(
            select.reshape(-1, local_count), tokens, preferred_element_type=jnp.float32
        ).astype(jnp.bfloat16)
        return rows.reshape(experts, places.shape[0], model_width)

    eight = jnp.arange(8, dtype=jnp.int32)
    outgoing_a = picked(eight)
    last = picked(16 + eight % 4)
    last = jnp.where(eight[None, :, None] < 4, last[:, :, :half], last[:, :, half:])
    outgoing_b = jnp.concatenate([picked(8 + eight), last], axis=2)

    packed, outgoing_a, outgoing_b, down_own, rank, gate_of, gu_scale, down_scale = (
        lax.optimization_barrier(
            (packed, outgoing_a, outgoing_b, down_own, rank, gate_of, gu_scale, down_scale)
        )
    )
    gu_own = exchange(packed)
    gu_own, outgoing_b = lax.optimization_barrier((gu_own, outgoing_b))
    gu_other = lax.ppermute(gu_own, "expert", swap)
    arrived_b = exchange(outgoing_b)
    arrived_b, gu_other, down_own, outgoing_a = lax.optimization_barrier(
        (arrived_b, gu_other, down_own, outgoing_a)
    )
    arrived_a = exchange(outgoing_a)
    down_other = lax.ppermute(down_own, "expert", swap)
    w_gu = dequantize_gu(gu_own, gu_other, gu_scale, parity)
    w_down = dequantize_down(down_own, down_other, down_scale, parity)
    produced = run_expert(arrived_b, w_gu, w_down, model_width)
    produced, arrived_a = lax.optimization_barrier((produced, arrived_a))
    produced = run_expert(arrived_a, w_gu, w_down, 0, produced)
    returned = exchange(produced)
    layer_out, grad = combine(returned, rank, gate_of, cotangent)
    gate_grad = jnp.sum(jnp.where(named, grad[None], 0.0), axis=1).T
    return (layer_out, gate_grad)


def solution(mesh):
    in_specs = (
        P("expert", None),
        P("expert", None),
        P("expert", None),
        P("expert", None),
        P(),
        P(None, "expert", None),
        P(),
        P(None, "expert", None),
        P(),
    )
    out_specs = (P("expert", None), P("expert", None))
    return jax.shard_map(shards, mesh=mesh, in_specs=in_specs, out_specs=out_specs, check_vma=False)
```

time: 565 us -> 440 us (0.78)
  waiting for transfers between devices: 384 us -> 7.33 us
  blocking collectives: 0 us -> 287 us
  starting transfers between devices: 60.5 us -> 18.3 us
  local copies, waits for them, and re-layouts: 20.1 us -> 38 us
  Pallas kernels: 83 us -> 73.3 us
    all_to_all x3 -> x2, waiting for transfers between devices: 384 us -> 7.33 us  [exchange(): lax.all_to_all(x, 'expert', 0, 0, axis_index_groups=same_core, tiled=True)]
    all_to_all x0 -> x3, blocking collectives: none -> 287 us  [exchange(): lax.all_to_all(x, 'expert', 0, 0, axis_index_groups=same_core, tiled=True)]
    all_to_all x3 -> x2, starting transfers between devices: 60.5 us -> 18.3 us  [exchange(): lax.all_to_all(x, 'expert', 0, 0, axis_index_groups=same_core, tiled=True)]
    unnamed x27 -> x39, local copies, waits for them, and re-layouts: 11.4 us -> 22.1 us
    pallas_call x1, Pallas kernels: 25.3 us -> 14.9 us  [dequantize_gu(): pl.pallas_call(gu_kernel, grid=(chips // 2,), in_specs=[pl.BlockSpec(memo...]
    dynamic_slice x2 -> x4, local copies, waits for them, and re-layouts: 0.21 us -> 7.32 us  [the longest x1 3.97 us: shards(): lax.dynamic_slice_in_dim(gu_payload, 4 * core + 8 * g, 8, axis=1)]
    pallas_call x3 -> x4, Pallas kernels: 57.7 us -> 58.5 us  [the longest x2 45 us: run_expert(): pl.pallas_call(functools.partial(expert_kernel, place), grid=(peers // gr...]
  transfers between devices with their start and end apart: 4 -> 4, of which waited for: 3 -> 1; matrix products, arithmetic and copies ran while one was open for 2% -> 9% of each run, Pallas kernels for 6% -> 11%
where the time goes in v3:
time: 440 us; the launch traced here: 438 us
  blocking collectives  287 us (65%)
  Pallas kernels  73.3 us (17%)
  local copies, waits for them, and re-layouts  38 us (9%)
  starting transfers between devices  18.3 us (4%)
  other arithmetic  8.21 us (2%)
  waiting for transfers between devices  7.33 us (2%)
  matrix products  5.44 us (1%)
    all_to_all x3, blocking collectives, exchange(): lax.all_to_all(x, 'expert', 0, 0, axis_index_groups=same_core, tiled=True)  287 us
    pallas_call x2, Pallas kernels, run_expert(): pl.pallas_call(functools.partial(expert_kernel, place), grid=(peers // gr...  45 us
    unnamed x39, local copies, waits for them, and re-layouts  22.1 us
    all_to_all x2, starting transfers between devices, exchange(): lax.all_to_all(x, 'expert', 0, 0, axis_index_groups=same_core, tiled=True)  18.3 us
    pallas_call x1, Pallas kernels, dequantize_gu(): pl.pallas_call(gu_kernel, grid=(chips // 2,), in_specs=[pl.BlockSpec(memo...  14.9 us
  transfers between devices with their start and end apart: 4, of which 1 were waited for; matrix products, arithmetic and copies ran while one was open for 9% of the time, Pallas kernels for 11%

profile of v3, /device:TPU:0, one launch (start us, length us, event | category | flops | bytes accessed | tf_op | source)
XLA Modules:
  0.0 438.2 jit_solution(6851456775719190844)
XLA Ops:
  0.6 0.0 copy-start
  0.6 11.9 %all-to-all-start = ((bf16[64,8,3584]{2,1,0:T(8,128)(2,1)}), bf16[64,8,3584]{2,1,0:T(8,128)(2,1)}, u32[]{:S(2)}, u32[]{:S(2)}) async-start(bf16[64,8,3584]{2,1,0:T(8,128)(2,1)} %param.16), calls=%async_computation | async-start | bytes 7340032 | tf_op jit(solution)/shard_map/all_to_all | solution.py:323
  12.6 7.6 %fusion.12 = (bf16[64,28,1024]{2,0,1:T(8,128)(2,1)}, bf16[64,28,1024]{2,0,1:T(8,128)(2,1)}) fusion(bf16[64,28,2048]{2,0,1:T(8,128)(2,1)} %param.14), kind=kLoop, calls=%fused_computation.40 | loop fusion | bytes 14680064 | tf_op jit(solution)/shard_map/slice | solution.py:331
  20.2 1.3 constant_dynamic-slice_fusion.2
  21.5 1.2 copy.41
  22.7 1.3 copy.39
  24.0 4.0 constant_dynamic-slice_fusion.6
  28.0 0.0 copy-start.13
  28.0 0.0 copy-start.15
  28.0 0.0 copy-start.14
  28.0 1.2 copy.37
  29.2 2.5 copy.36
  31.7 2.5 copy.35
  34.1 0.1 eq.91
  34.2 0.0 copy-done.13
  34.2 0.0 copy-done.15
  34.2 0.1 select_reduce_fusion.2
  34.4 0.1 fusion.3.rank_ref
  34.5 0.1 eq.99
  34.6 0.1 eq.95
  34.7 0.0 copy-done.14
  34.8 1.1 constant_dynamic-slice_fusion
  35.9 0.2 copy.44
  36.1 0.1 broadcast_in_dim.73
  36.3 0.1 copy.46
  36.4 1.0 constant_dynamic-slice_fusion.1
  37.4 0.2 copy.45
  37.6 0.0 copy-done
  37.6 3.0 fusion
  40.6 1.2 fusion.2
  41.8 1.2 fusion.1
  42.9 0.2 slice_select_fusion
  43.2 0.0 copy-start.11
  43.2 0.0 copy-start.12
  43.2 3.2 pad_maximum_fusion
  46.4 0.1 broadcast_bitcast_fusion.scale_ref
  46.5 0.9 copy-done.10
  47.4 0.1 copy-done.11
  47.5 0.2 copy-done.12
  47.6 4.0 maximum_maximum_fusion
  51.6 7.3 %all-to-all-done.own_ref = bf16[64,8,3584]{2,1,0:T(8,128)(2,1)} async-done(((bf16[64,8,3584]{2,1,0:T(8,128)(2,1)}), bf16[64,8,3584]{2,1,0:T(8,128)(2,1)}, u32[]{:S(2)}, u32[]{:S(2)}) %all-to-all-start) | async-done | bytes 3670048 | tf_op jit(solution)/shard_map/all_to_all | solution.py:323
  59.0 96.7 %all_to_all.25.own_ref = bf16[64,8,7168]{2,1,0:T(8,128)(2,1)S(1)} all-to-all(bf16[64,8,7168]{2,1,0:T(8,128)(2,1)} %maximum_maximum_fusion), channel_id=1, replica_groups={{0,2,4,6,8,10,12,14,16,18,20,22,24,26,28,30,32,34,36,38,40,42,44,46,48,..., dimensions={0} | all-to-all | bytes 14680064 | tf_op jit(solution)/shard_map/all_to_all | solution.py:323
  155.7 0.0 collective-permute-start
  155.7 0.0 copy-done.8
  155.7 73.7 %all_to_all.26.x_ref = bf16[64,8,5376]{2,1,0:T(8,128)(2,1)} all-to-all(bf16[64,8,5376]{2,1,0:T(8,128)(2,1)S(1)} %copy-done.8), channel_id=1, replica_groups={{0,2,4,6,8,10,12,14,16,18,20,22,24,26,28,30,32,34,36,38,40,42,44,46,48,..., dimensions={0} | all-to-all | bytes 11010048 | tf_op jit(solution)/shard_map/all_to_all | solution.py:323
  229.3 0.0 collective-permute-done.other_ref
  229.3 3.0 copy-done.5
  232.3 0.0 collective-permute-start.1
  232.4 6.5 %all-to-all-start.3 = ((bf16[64,8,3584]{2,1,0:T(8,128)(2,1)}), bf16[64,8,3584]{2,1,0:T(8,128)(2,1)}, u32[]{:S(2)}, u32[]{:S(2)}) async-start(bf16[64,8,3584]{2,1,0:T(8,128)(2,1)} %fusion), calls=%async_computation.3 | async-start | bytes 7340032 | tf_op jit(solution)/shard_map/all_to_all | solution.py:323
  238.8 3.1 copy-done.3
  241.9 3.1 copy-done.6
  245.0 14.9 %dequantize_gu.1.gu_hbm = bf16[3584,2048]{1,0:T(8,128)(2,1)} custom-call(s32[1]{0:T(128)} %bitcast.9.parity_ref, bf16[64,8,7168]{2,1,0:T(8,128)(2,1)S(1)} %copy-done.3, bf16[64,8,7168]{2,1,0:T(8,128)(2,1)S(1)} %copy-done.6, f32[28,2048]{1,0:T(8,128)S(1)} %bitcast.31), custom_call_target="tpu_custom_call" | custom-call | flops 7340032 | bytes 29360128 | tf_op jit(solution)/shard_map/dequantize_gu/pallas_call | solution.py:64
  259.8 0.0 collective-permute-done.1.other_ref
  259.8 5.8 %dequantize_down.1.down_hbm = bf16[1024,3584]{1,0:T(8,128)(2,1)S(1)} custom-call(s32[1]{0:T(128)} %bitcast.9.parity_ref, bf16[64,8,3584]{2,1,0:T(8,128)(2,1)} %all-to-all-done.own_ref, bf16[64,8,3584]{2,1,0:T(8,128)(2,1)} %collective-permute-done.1.other_ref, f32[8,3584]{1,0:T(8,128)S(1)} %broadcast_bitcast_fusion.scale_ref), custom_call_target="tpu_custom_call" | custom-call | flops 3670016 | bytes 14680064 | tf_op jit(solution)/shard_map/dequantize_down/pallas_call | solution.py:100
  265.7 0.0 copy-start.4
  265.7 3.0 copy-done.4
  268.7 25.5 %run_expert.2.refs_0_ = bf16[64,8,8960]{2,1,0:T(8,128)(2,1)} custom-call(bf16[64,8,5376]{2,1,0:T(8,128)(2,1)} %all_to_all.26.x_ref, bf16[3584,2048]{1,0:T(8,128)(2,1)} %dequantize_gu.1.gu_hbm, bf16[1024,3584]{1,0:T(8,128)(2,1)} %copy-done.4), custom_call_target="tpu_custom_call" | custom-call | flops 16911433728 | bytes 33030144 | tf_op jit(solution)/shard_map/run_expert/pallas_call | solution.py:208
  294.2 0.0 all-to-all-done.3.x_ref
  294.2 19.5 %run_expert.3 = bf16[64,8,8960]{2,1,0:T(8,128)(2,1)} custom-call(bf16[64,8,3584]{2,1,0:T(8,128)(2,1)} %all-to-all-done.3.x_ref, bf16[3584,2048]{1,0:T(8,128)(2,1)} %dequantize_gu.1.gu_hbm, bf16[1024,3584]{1,0:T(8,128)(2,1)} %copy-done.4, bf16[64,8,8960]{2,1,0:T(8,128)(2,1)} %run_expert.2.refs_0_), custom_call_target="tpu_custom_call", output_to_operand_aliasing={{}: (3, {})} | custom-call | flops 11274289152 | bytes 29360128 | tf_op jit(solution)/shard_map/run_expert/pallas_call | solution.py:208
  313.7 0.0 copy-start.7
  313.7 0.0 copy-start.1
  313.7 116.1 %all_to_all.27.x_ref = bf16[64,8,8960]{2,1,0:T(8,128)(2,1)S(1)} all-to-all(bf16[64,8,8960]{2,1,0:T(8,128)(2,1)} %run_expert.3), channel_id=1, replica_groups={{0,2,4,6,8,10,12,14,16,18,20,22,24,26,28,30,32,34,36,38,40,42,44,46,48,..., dimensions={0} | all-to-all | bytes 18350080 | tf_op jit(solution)/shard_map/all_to_all | solution.py:323
  429.9 7.7 %combine.1 = (bf16[128,3584]{1,0:T(8,128)(2,1)}, f32[64,128]{1,0:T(8,128)S(1)}) custom-call(bf16[64,8,8960]{2,1,0:T(8,128)(2,1)S(1)} %all_to_all.27.x_ref, s32[64,128]{1,0:T(8,128)S(1)} %fusion.3.rank_ref, f32[64,128]{1,0:T(8,128)S(1)} %select_reduce_fusion.1.gate_ref, bf16[128,3584]{1,0:T(8,128)(2,1)S(1)} %copy-done.7), custom_call_target="tpu_custom_call" | custom-call | flops 2818572288 | bytes 11010048 | tf_op jit(solution)/shard_map/combine/pallas_call | solution.py:281
  437.6 0.6 select_reduce_fusion
  (21 shorter events, 0.1 us)
Async XLA Ops:
  0.6 37.0 %copy-start = (bf16[128,3584]{1,0:T(8,128)(2,1)S(1)}, bf16[128,3584]{1,0:T(8,128)(2,1)}, u32[]{:S(2)}) copy-start(bf16[128,3584]{1,0:T(8,128)(2,1)} %param.9) | copy-start | bytes 2752516
  0.6 58.3 %all-to-all-start = ((bf16[64,8,3584]{2,1,0:T(8,128)(2,1)}), bf16[64,8,3584]{2,1,0:T(8,128)(2,1)}, u32[]{:S(2)}, u32[]{:S(2)}) async-start(bf16[64,8,3584]{2,1,0:T(8,128)(2,1)} %param.16), calls=%async_computation | async-start | bytes 7340032 | tf_op jit(solution)/shard_map/all_to_all | solution.py:323
  28.0 6.3 %copy-start.13 = (s32[128,8]{0,1:T(8,128)S(1)}, s32[128,8]{0,1:T(8,128)}, u32[]{:S(2)}) copy-start(s32[128,8]{0,1:T(8,128)} %param.11) | copy-start | bytes 12292
  28.0 6.3 %copy-start.15 = (s32[64]{0:T(128)S(1)}, s32[64]{0:T(128)}, u32[]{:S(2)}) copy-start(s32[64]{0:T(128)} %param.13) | copy-start | bytes 772
  28.0 6.7 %copy-start.14 = (bf16[128,8]{0,1:T(8,128)(2,1)S(1)}, bf16[128,8]{0,1:T(8,128)(2,1)}, u32[]{:S(2)}) copy-start(bf16[128,8]{0,1:T(8,128)(2,1)} %param.12) | copy-start | bytes 6148
  43.2 3.3 copy-start.9
  43.2 4.2 copy-start.10
  43.2 4.3 copy-start.11
  43.2 4.4 %copy-start.12 = (bf16[64,4,1024]{2,1,0:T(4,128)(2,1)S(1)}, bf16[64,4,1024]{2,1,0:T(4,128)(2,1)}, u32[]{:S(2)}) copy-start(bf16[64,4,1024]{2,1,0:T(4,128)(2,1)} %copy.39) | copy-start | bytes 1572868
  59.0 96.7 %copy-start.8 = (bf16[64,8,5376]{2,1,0:T(8,128)(2,1)S(1)}, bf16[64,8,5376]{2,1,0:T(8,128)(2,1)}, u32[]{:S(2)}) copy-start(bf16[64,8,5376]{2,1,0:T(8,128)(2,1)} %pad_maximum_fusion) | copy-start | bytes 16515076
  155.7 73.7 %copy-start.2 = (bf16[64,8,7168]{2,1,0:T(8,128)(2,1)}, bf16[64,8,7168]{2,1,0:T(8,128)(2,1)S(1)}, u32[]{:S(2)}) copy-start(bf16[64,8,7168]{2,1,0:T(8,128)(2,1)S(1)} %all_to_all.25.own_ref) | copy-start | bytes 22020100
  155.7 73.7 %collective-permute-start = (bf16[64,8,7168]{2,1,0:T(8,128)(2,1)S(1)}, bf16[64,8,7168]{2,1,0:T(8,128)(2,1)S(1)}, u32[]{:S(2)}, u32[]{:S(2)}) collective-permute-start(bf16[64,8,7168]{2,1,0:T(8,128)(2,1)S(1)} %all_to_all.25.own_ref), channel_id=1, source_target_pairs={{0,1},{1,0},{2,3},{3,2},{4,5},{5,4},{6,7},{7,6},{8,9},{9,8},{10,11... | collective-permute-start | bytes 22020104 | tf_op jit(solution)/shard_map/ppermute | solution.py:377
  229.3 3.0 copy-start.5
  232.3 27.5 %collective-permute-start.1 = (bf16[64,8,3584]{2,1,0:T(8,128)(2,1)}, bf16[64,8,3584]{2,1,0:T(8,128)(2,1)}, u32[]{:S(2)}, u32[]{:S(2)}) collective-permute-start(bf16[64,8,3584]{2,1,0:T(8,128)(2,1)} %all-to-all-done.own_ref), channel_id=1, source_target_pairs={{0,1},{1,0},{2,3},{3,2},{4,5},{5,4},{6,7},{7,6},{8,9},{9,8},{10,11... | collective-permute-start | bytes 11010056 | tf_op jit(solution)/shard_map/ppermute | solution.py:383
  232.4 61.8 %all-to-all-start.3 = ((bf16[64,8,3584]{2,1,0:T(8,128)(2,1)}), bf16[64,8,3584]{2,1,0:T(8,128)(2,1)}, u32[]{:S(2)}, u32[]{:S(2)}) async-start(bf16[64,8,3584]{2,1,0:T(8,128)(2,1)} %fusion), calls=%async_computation.3 | async-start | bytes 7340032 | tf_op jit(solution)/shard_map/all_to_all | solution.py:323
  238.8 3.1 copy-start.3
  241.9 3.1 copy-start.6
  265.7 3.0 copy-start.4
  313.7 116.2 %copy-start.7 = (bf16[128,3584]{1,0:T(8,128)(2,1)S(1)}, bf16[128,3584]{1,0:T(8,128)(2,1)}, u32[]{:S(2)}) copy-start(bf16[128,3584]{1,0:T(8,128)(2,1)} %cotangent_ref.1) | copy-start | bytes 2752516
  313.7 124.5 %copy-start.1 = (bf16[128,3584]{1,0:T(8,128)(2,1)S(1)}, bf16[128,3584]{1,0:T(8,128)(2,1)}, u32[]{:S(2)}) copy-start(bf16[128,3584]{1,0:T(8,128)(2,1)} %param.9) | copy-start | bytes 2752516

commit v4 on v3

--- a/solution.py
+++ b/solution.py
@@ -17,127 +17,44 @@
     return block.astype(jnp.float32).reshape(-1, block.shape[-1]).astype(jnp.bfloat16)
 
 
-def by_core(parity_ref, own_ref, other_ref, body):
-    @pl.when(parity_ref[0] == 0)
-    def _():
-        body(own_ref, other_ref)
-
-    @pl.when(parity_ref[0] != 0)
-    def _():
-        body(other_ref, own_ref)
-
-
-def gu_kernel(parity_ref, own_ref, other_ref, scale_ref, out_ref):
-    step = pl.program_id(0)
-    width = out_ref.shape[1]
-
-    def body(zero_ref, one_ref):
-        tiles = []
-        for chip in range(zero_ref.shape[0]):
-            zero = [zero_ref[chip, :, g * width : (g + 1) * width] for g in range(3)]
-            one = [one_ref[chip, :, g * width : (g + 1) * width] for g in range(3)]
-            fold_zero = zero_ref[chip, :, 3 * width :].astype(jnp.float32)
-            fold_one = one_ref[chip, :, 3 * width :].astype(jnp.float32)
-            middle = jnp.concatenate(
-                [
-                    jnp.concatenate([fold_zero[:4], fold_one[:4]], axis=0),
-                    jnp.concatenate([fold_zero[4:], fold_one[4:]], axis=0),
-                ],
-                axis=1,
-            )
-            tiles += zero + [middle] + one
-        for pair in range(len(tiles) // 2):
-            scaled = []
-            for k in (2 * pair, 2 * pair + 1):
-                at = (step * 8 * len(tiles) + 8 * k) // 128
-                scaled.append(tiles[k].astype(jnp.float32) * scale_ref[pl.ds(at, 1), :])
-            out_ref[16 * pair : 16 * pair + 16, :] = jnp.concatenate(scaled, axis=0).astype(
-                jnp.bfloat16
-            )
-
-    by_core(parity_ref, own_ref, other_ref, body)
-
-
-def dequantize_gu(own, other, scales, parity):
-    chips, _, packed = own.shape
-    width = 2 * FF
-    return pl.pallas_call(
-        gu_kernel,
-        grid=(chips // 2,),
-        in_specs=[
-            pl.BlockSpec(memory_space=pltpu.SMEM),
-            pl.BlockSpec((2, 8, packed), lambda i: (i, 0, 0)),
-            pl.BlockSpec((2, 8, packed), lambda i: (i, 0, 0)),
-            pl.BlockSpec(scales.shape, lambda i: (0, 0)),
-        ],
-        out_specs=pl.BlockSpec((112, width), lambda i: (i, 0)),
-        out_shape=jax.ShapeDtypeStruct((chips * 56, width), jnp.bfloat16),
-        compiler_params=pltpu.CompilerParams(vmem_limit_bytes=32 * 1024 * 1024),
-        cost_estimate=pl.CostEstimate(
-            flops=chips * 56 * width, bytes_accessed=chips * 56 * width * 4, transcendentals=0
-        ),
-        name="dequantize_gu",
-    )(parity, own, other, scales)
-
-
-def down_kernel(parity_ref, own_ref, other_ref, scale_ref, out_ref):
-    step = pl.program_id(0)
-    chips = own_ref.shape[0]
-    scale = scale_ref[pl.ds(step * chips * 16 // 128, 1), :]
-
-    def body(zero_ref, one_ref):
-        for chip in range(chips):
-            both = [ref[chip].astype(jnp.float32) * scale for ref in (zero_ref, one_ref)]
-            out_ref[16 * chip : 16 * chip + 16, :] = jnp.concatenate(both, axis=0).astype(
-                jnp.bfloat16
-            )
-
-    by_core(parity_ref, own_ref, other_ref, body)
-
-
-def dequantize_down(own, other, scales, parity):
-    chips, _, width = own.shape
-    return pl.pallas_call(
-        down_kernel,
-        grid=(chips // 8,),
-        in_specs=[
-            pl.BlockSpec(memory_space=pltpu.SMEM),
-            pl.BlockSpec((8, 8, width), lambda i: (i, 0, 0)),
-            pl.BlockSpec((8, 8, width), lambda i: (i, 0, 0)),
-            pl.BlockSpec(scales.shape, lambda i: (0, 0)),
-        ],
-        out_specs=pl.BlockSpec((128, width), lambda i: (i, 0)),
-        out_shape=jax.ShapeDtypeStruct((chips * 16, width), jnp.bfloat16),
-        compiler_params=pltpu.CompilerParams(vmem_limit_bytes=32 * 1024 * 1024),
-        cost_estimate=pl.CostEstimate(
-            flops=chips * 16 * width, bytes_accessed=chips * 16 * width * 4, transcendentals=0
-        ),
-        name="dequantize_down",
-    )(parity, own, other, scales)
-
-
-def expert_kernel(place, x_ref, gu_hbm, down_hbm, *refs):
-    out_ref, gu_ref, down_ref, rows_ref, active_ref, sems = refs[-6:]
-    step = pl.program_id(0)
+def restore(zero_gu, one_gu, zero_down, one_down, gu_scale_ref, down_scale_ref, step, gu_ref, down_ref):
+    width = gu_ref.shape[1]
+    chips = zero_gu.shape[0]
+    tiles = []
+    for chip in range(chips):
+        zero = [zero_gu[chip, :, g * width : (g + 1) * width] for g in range(3)]
+        one = [one_gu[chip, :, g * width : (g + 1) * width] for g in range(3)]
+        fold_zero = zero_gu[chip, :, 3 * width :].astype(jnp.float32)
+        fold_one = one_gu[chip, :, 3 * width :].astype(jnp.float32)
+        middle = jnp.concatenate(
+            [
+                jnp.concatenate([fold_zero[:4], fold_one[:4]], axis=0),
+                jnp.concatenate([fold_zero[4:], fold_one[4:]], axis=0),
+            ],
+            axis=1,
+        )
+        tiles += zero + [middle] + one
+    for pair in range(len(tiles) // 2):
+        scaled = []
+        for k in (2 * pair, 2 * pair + 1):
+            at = (step * 8 * len(tiles) + 8 * k) // 128
+            scaled.append(tiles[k].astype(jnp.float32) * gu_scale_ref[pl.ds(at, 1), :])
+        start = pl.multiple_of(step * 8 * len(tiles) + 16 * pair, 16)
+        gu_ref[pl.ds(start, 16), :] = jnp.concatenate(scaled, axis=0).astype(jnp.bfloat16)
+    scale = down_scale_ref[pl.ds(step * chips * 16 // 128, 1), :]
+    for chip in range(chips):
+        both = [ref[chip].astype(jnp.float32) * scale for ref in (zero_down, one_down)]
+        start = pl.multiple_of((step * chips + chip) * 16, 16)
+        down_ref[pl.ds(start, 16), :] = jnp.concatenate(both, axis=0).astype(jnp.bfloat16)
+
+
+def expert_rows(place, x_ref, out_ref, gu_ref, down_ref, rows_ref, active_ref, ready):
     peers, _, packed = x_ref.shape
     width = rows_ref.shape[1]
     half = width // 2
     full = packed // width
     eight = 8 * peers
     chunks = FF // COLS
-    copies = []
-    for j in range(chunks):
-        for start in (j * COLS, FF + j * COLS):
-            part = (slice(None), pl.ds(start, COLS))
-            copies.append(
-                pltpu.make_async_copy(gu_hbm.at[part], gu_ref.at[part], sems.at[len(copies)])
-            )
-    copies.append(pltpu.make_async_copy(down_hbm, down_ref, sems.at[len(copies)]))
-
-    @pl.when(step == 0)
-    def _():
-        for copy in copies:
-            copy.start()
 
     for q in range(0, peers, 4):
         for g in range(full):
@@ -152,12 +69,7 @@
                 ).astype(jnp.bfloat16)
 
     for j in range(chunks):
-
-        @pl.when(step == 0)
-        def _():
-            copies[2 * j].wait()
-            copies[2 * j + 1].wait()
-
+        ready(j)
         gate = jnp.dot(
             rows_ref[...], gu_ref[:, j * COLS : (j + 1) * COLS], preferred_element_type=jnp.float32
         )
@@ -169,10 +81,7 @@
         active_ref[:, j * COLS : (j + 1) * COLS] = (gate / (1.0 + jnp.exp(-gate)) * up).astype(
             jnp.bfloat16
         )
-
-    @pl.when(step == 0)
-    def _():
-        copies[-1].wait()
+    ready(chunks)
 
     for j in range(half // COLS):
         sides = []
@@ -196,27 +105,130 @@
                 ).astype(jnp.bfloat16)
 
 
-def run_expert(arrived, w_gu, w_down, place, produced=None):
+def first_kernel(place, parity_ref, own_gu, other_gu, own_down, other_down, gu_scale_ref, down_scale_ref, x_ref, out_ref, gu_hbm, down_hbm, gu_ref, down_ref, rows_ref, active_ref, sems):
+    step = pl.program_id(0)
+    restoring = gu_ref.shape[0] // (56 * own_gu.shape[0])
+    scales = (gu_scale_ref, down_scale_ref)
+
+    @pl.when((step < restoring) & (parity_ref[0] == 0))
+    def _():
+        restore(own_gu, other_gu, own_down, other_down, *scales, step, gu_ref, down_ref)
+
+    @pl.when((step < restoring) & (parity_ref[0] != 0))
+    def _():
+        restore(other_gu, own_gu, other_down, own_down, *scales, step, gu_ref, down_ref)
+
+    leaving = [
+        pltpu.make_async_copy(gu_ref, gu_hbm, sems.at[0]),
+        pltpu.make_async_copy(down_ref, down_hbm, sems.at[1]),
+    ]
+
+    @pl.when(step == restoring)
+    def _():
+        for copy in leaving:
+            copy.start()
+
+    @pl.when(step >= restoring)
+    def _():
+        expert_rows(place, x_ref, out_ref, gu_ref, down_ref, rows_ref, active_ref, lambda j: None)
+
+    @pl.when(step == pl.num_programs(0) - 1)
+    def _():
+        for copy in leaving:
+            copy.wait()
+
+
+def run_first(arrived, own_gu, other_gu, own_down, other_down, gu_scale, down_scale, parity, place):
+    peers, _, packed = arrived.shape
+    width = down_scale.shape[1]
+    each = 8 * packed // width
+    total = width * 5 // 2
+    group, chips = 32, 4
+    restoring = peers // chips
+    rows = peers * each
+
+    def part(count):
+        return pl.BlockSpec((chips, 8, count), lambda i: (jnp.minimum(i, restoring - 1), 0, 0))
+
+    def piece(count):
+        return pl.BlockSpec((group, 8, count), lambda i: (jnp.maximum(i - restoring, 0), 0, 0))
+
+    gu_shape, down_shape = (width, 2 * FF), (FF, width)
+    return pl.pallas_call(
+        functools.partial(first_kernel, place),
+        grid=(restoring + peers // group,),
+        in_specs=[
+            pl.BlockSpec(memory_space=pltpu.SMEM),
+            part(own_gu.shape[2]),
+            part(own_gu.shape[2]),
+            part(width),
+            part(width),
+            pl.BlockSpec(gu_scale.shape, lambda i: (0, 0)),
+            pl.BlockSpec(down_scale.shape, lambda i: (0, 0)),
+            piece(packed),
+        ],
+        out_specs=[piece(total), pl.BlockSpec(memory_space=pl.ANY), pl.BlockSpec(memory_space=pl.ANY)],
+        out_shape=[
+            jax.ShapeDtypeStruct((peers, 8, total), jnp.bfloat16),
+            jax.ShapeDtypeStruct(gu_shape, jnp.bfloat16),
+            jax.ShapeDtypeStruct(down_shape, jnp.bfloat16),
+        ],
+        scratch_shapes=[
+            pltpu.VMEM(gu_shape, jnp.bfloat16),
+            pltpu.VMEM(down_shape, jnp.bfloat16),
+            pltpu.VMEM((group * each, width), jnp.bfloat16),
+            pltpu.VMEM((group * each, FF), jnp.bfloat16),
+            pltpu.SemaphoreType.DMA((2,)),
+        ],
+        compiler_params=pltpu.CompilerParams(vmem_limit_bytes=56 * 1024 * 1024),
+        cost_estimate=pl.CostEstimate(
+            flops=rows * width * FF * 6,
+            bytes_accessed=rows * width * 4 + width * FF * 12,
+            transcendentals=rows * FF,
+        ),
+        name="restore_and_run",
+    )(parity, own_gu, other_gu, own_down, other_down, gu_scale, down_scale, arrived)
+
+
+def expert_kernel(x_ref, gu_hbm, down_hbm, produced, out_ref, gu_ref, down_ref, rows_ref, active_ref, sems):
+    step = pl.program_id(0)
+    copies = []
+    for j in range(FF // COLS):
+        for start in (j * COLS, FF + j * COLS):
+            part = (slice(None), pl.ds(start, COLS))
+            copies.append(
+                pltpu.make_async_copy(gu_hbm.at[part], gu_ref.at[part], sems.at[len(copies)])
+            )
+    copies.append(pltpu.make_async_copy(down_hbm, down_ref, sems.at[len(copies)]))
+
+    @pl.when(step == 0)
+    def _():
+        for copy in copies:
+            copy.start()
+
+    def ready(j):
+        @pl.when(step == 0)
+        def _():
+            for copy in copies[2 * j : 2 * j + 2]:
+                copy.wait()
+
+    expert_rows(0, x_ref, out_ref, gu_ref, down_ref, rows_ref, active_ref, ready)
+
+
+def run_expert(arrived, w_gu, w_down, produced):
     peers, _, packed = arrived.shape
     width = w_gu.shape[0]
     each = 8 * packed // width
-    group = 32
+    group = 64
     rows = peers * each
-    total = width * 5 // 2
-    columns = total if produced is None else packed
-    before = () if produced is None else (produced,)
+    piece = pl.BlockSpec((group, 8, packed), lambda i: (i, 0, 0))
     return pl.pallas_call(
-        functools.partial(expert_kernel, place),
+        expert_kernel,
         grid=(peers // group,),
-        in_specs=[
-            pl.BlockSpec((group, 8, packed), lambda i: (i, 0, 0)),
-            pl.BlockSpec(memory_space=pl.ANY),
-            pl.BlockSpec(memory_space=pl.ANY),
-        ]
-        + [pl.BlockSpec(memory_space=pl.ANY)] * len(before),
-        out_specs=pl.BlockSpec((group, 8, columns), lambda i: (i, 0, 0)),
-        out_shape=jax.ShapeDtypeStruct((peers, 8, total), jnp.bfloat16),
-        input_output_aliases={3: 0} if before else {},
+        in_specs=[piece] + [pl.BlockSpec(memory_space=pl.ANY)] * 3,
+        out_specs=piece,
+        out_shape=jax.ShapeDtypeStruct(produced.shape, jnp.bfloat16),
+        input_output_aliases={3: 0},
         scratch_shapes=[
             pltpu.VMEM(w_gu.shape, jnp.bfloat16),
             pltpu.VMEM(w_down.shape, jnp.bfloat16),
@@ -231,7 +243,7 @@
             transcendentals=rows * FF,
         ),
         name="run_expert",
-    )(arrived, w_gu, w_down, *before)
+    )(arrived, w_gu, w_down, produced)
 
 
 def combine_kernel(x_ref, rank_ref, gate_ref, cotangent_ref, out_ref, grad_ref, sum_ref):
@@ -381,11 +393,11 @@
     )
     arrived_a = exchange(outgoing_a)
     down_other = lax.ppermute(down_own, "expert", swap)
-    w_gu = dequantize_gu(gu_own, gu_other, gu_scale, parity)
-    w_down = dequantize_down(down_own, down_other, down_scale, parity)
-    produced = run_expert(arrived_b, w_gu, w_down, model_width)
+    produced, w_gu, w_down = run_first(
+        arrived_b, gu_own, gu_other, down_own, down_other, gu_scale, down_scale, parity, model_width
+    )
     produced, arrived_a = lax.optimization_barrier((produced, arrived_a))
-    produced = run_expert(arrived_a, w_gu, w_down, 0, produced)
+    produced = run_expert(arrived_a, w_gu, w_down, produced)
     returned = exchange(produced)
     layer_out, grad = combine(returned, rank, gate_of, cotangent)
     gate_grad = jnp.sum(jnp.where(named, grad[None], 0.0), axis=1).T

time: 440 us -> 432 us (0.982)
  waiting for transfers between devices: 7.33 us -> 22 us
  local copies, waits for them, and re-layouts: 38 us -> 25.7 us
  Pallas kernels: 73.3 us -> 61.8 us
    all_to_all x2, waiting for transfers between devices: 7.33 us -> 21.7 us  [exchange(): lax.all_to_all(x, 'expert', 0, 0, axis_index_groups=same_core, tiled=True)]
    pallas_call x4 -> x2, Pallas kernels: 65.6 us -> 54.1 us  [the longest x1 35.8 us: run_first(): pl.pallas_call(functools.partial(first_kernel, place), grid=(restoring +...]
    unnamed x39 -> x33, local copies, waits for them, and re-layouts: 22.1 us -> 11 us
  transfers between devices with their start and end apart: 4 -> 4, of which waited for: 1 -> 3; matrix products, arithmetic and copies ran while one was open for 9% -> 8% of each run, Pallas kernels for 11% -> 8%
where the time goes in v4:
time: 432 us; the launch traced here: 431 us
  blocking collectives  288 us (67%)
  Pallas kernels  61.8 us (14%)
  local copies, waits for them, and re-layouts  25.7 us (6%)
  waiting for transfers between devices  22 us (5%)
  starting transfers between devices  18.3 us (4%)
  other arithmetic  8.18 us (2%)
  matrix products  5.41 us (1%)
    all_to_all x3, blocking collectives, exchange(): lax.all_to_all(x, 'expert', 0, 0, axis_index_groups=same_core, tiled=True)  288 us
    pallas_call x1, Pallas kernels, run_first(): pl.pallas_call(functools.partial(first_kernel, place), grid=(restoring +...  35.8 us
    all_to_all x2, waiting for transfers between devices, exchange(): lax.all_to_all(x, 'expert', 0, 0, axis_index_groups=same_core, tiled=True)  21.7 us
    all_to_all x2, starting transfers between devices, exchange(): lax.all_to_all(x, 'expert', 0, 0, axis_index_groups=same_core, tiled=True)  18.3 us
    pallas_call x1, Pallas kernels, run_expert(): pl.pallas_call(expert_kernel, grid=(peers // group,), in_specs=[piece] +...  18.3 us
    unnamed x33, local copies, waits for them, and re-layouts  11 us
  transfers between devices with their start and end apart: 4, of which 3 were waited for; matrix products, arithmetic and copies ran while one was open for 8% of the time, Pallas kernels for 8%

profile of v4, /device:TPU:0, one launch (start us, length us, event | category | flops | bytes accessed | tf_op | source)
XLA Modules:
  0.0 430.9 jit_solution(6620283485388298203)
XLA Ops:
  0.6 0.0 copy-start
  0.6 0.0 copy-start.10
  0.7 0.0 copy-start.11
  0.7 0.0 copy-start.9
  0.7 0.0 copy-start.8
  0.7 0.0 copy-start.7
  0.7 11.9 %all-to-all-start = ((bf16[64,8,3584]{2,1,0:T(8,128)(2,1)}), bf16[64,8,3584]{2,1,0:T(8,128)(2,1)}, u32[]{:S(2)}, u32[]{:S(2)}) async-start(bf16[64,8,3584]{2,1,0:T(8,128)(2,1)} %param.16), calls=%async_computation | async-start | bytes 7340032 | tf_op jit(solution)/shard_map/all_to_all | solution.py:335
  12.7 0.0 copy-done.10
  12.7 0.0 copy-done.11
  12.7 0.0 copy-done.9
  12.7 0.1 select_reduce_fusion.2
  12.9 0.1 fusion.3.rank_ref
  13.0 0.1 eq.99
  13.1 0.1 eq.95
  13.2 0.1 eq.91
  13.3 0.0 copy-done.8
  13.4 0.1 constant_dynamic-slice_fusion.1
  13.4 0.2 copy.45
  13.7 0.0 copy-done.7
  13.7 0.1 constant_dynamic-slice_fusion
  13.8 0.2 copy.44
  14.1 0.1 broadcast_in_dim.73
  14.3 0.8 copy.46
  15.0 7.6 %fusion.12 = (bf16[64,28,1024]{2,0,1:T(8,128)(2,1)}, bf16[64,28,1024]{2,0,1:T(8,128)(2,1)}) fusion(bf16[64,28,2048]{2,0,1:T(8,128)(2,1)} %param.14), kind=kLoop, calls=%fused_computation.40 | loop fusion | bytes 14680064 | tf_op jit(solution)/shard_map/slice | solution.py:343
  22.7 4.0 constant_dynamic-slice_fusion.6
  26.6 1.2 copy.35
  27.8 2.5 copy.37
  30.3 2.5 copy.36
  32.7 1.3 constant_dynamic-slice_fusion.2
  34.0 0.4 copy.41
  34.4 0.4 copy.39
  34.8 0.0 copy-done
  34.8 3.0 fusion
  37.8 1.2 fusion.1
  39.0 1.2 fusion.2
  40.1 0.2 slice_select_fusion
  40.4 0.0 copy-start.4
  40.4 0.0 copy-start.5
  40.4 3.2 pad_maximum_fusion
  43.5 0.7 broadcast_bitcast_fusion.down_scale_ref
  44.3 0.0 copy-done.4
  44.3 0.3 copy-done.5
  44.6 4.0 maximum_maximum_fusion
  48.5 10.5 %all-to-all-done.own_down = bf16[64,8,3584]{2,1,0:T(8,128)(2,1)} async-done(((bf16[64,8,3584]{2,1,0:T(8,128)(2,1)}), bf16[64,8,3584]{2,1,0:T(8,128)(2,1)}, u32[]{:S(2)}, u32[]{:S(2)}) %all-to-all-start) | async-done | bytes 3670048 | tf_op jit(solution)/shard_map/all_to_all | solution.py:335
  59.0 96.7 %all_to_all.25.own_gu = bf16[64,8,7168]{2,1,0:T(8,128)(2,1)S(1)} all-to-all(bf16[64,8,7168]{2,1,0:T(8,128)(2,1)} %maximum_maximum_fusion), channel_id=1, replica_groups={{0,2,4,6,8,10,12,14,16,18,20,22,24,26,28,30,32,34,36,38,40,42,44,46,48,..., dimensions={0} | all-to-all | bytes 14680064 | tf_op jit(solution)/shard_map/all_to_all | solution.py:335
  155.7 0.0 collective-permute-start
  155.7 0.0 copy-done.3
  155.7 73.7 %all_to_all.26.x_ref = bf16[64,8,5376]{2,1,0:T(8,128)(2,1)} all-to-all(bf16[64,8,5376]{2,1,0:T(8,128)(2,1)S(1)} %copy-done.3), channel_id=1, replica_groups={{0,2,4,6,8,10,12,14,16,18,20,22,24,26,28,30,32,34,36,38,40,42,44,46,48,..., dimensions={0} | all-to-all | bytes 11010048 | tf_op jit(solution)/shard_map/all_to_all | solution.py:335
  229.4 0.0 copy-done.6
  229.4 0.0 collective-permute-done.other_gu
  229.4 2.9 copy-done.12
  232.3 0.0 collective-permute-start.1
  232.3 6.5 %all-to-all-start.3 = ((bf16[64,8,3584]{2,1,0:T(8,128)(2,1)}), bf16[64,8,3584]{2,1,0:T(8,128)(2,1)}, u32[]{:S(2)}, u32[]{:S(2)}) async-start(bf16[64,8,3584]{2,1,0:T(8,128)(2,1)} %fusion), calls=%async_computation.3 | async-start | bytes 7340032 | tf_op jit(solution)/shard_map/all_to_all | solution.py:335
  238.8 0.3 collective-permute-done.1.other_down
  239.1 35.8 %restore_and_run.1 = (bf16[64,8,8960]{2,1,0:T(8,128)(2,1)}, bf16[3584,2048]{1,0:T(8,128)(2,1)}, bf16[1024,3584]{1,0:T(8,128)(2,1)}) custom-call(s32[1]{0:T(128)} %bitcast.parity_ref, bf16[64,8,7168]{2,1,0:T(8,128)(2,1)} %copy-done.6, bf16[64,8,7168]{2,1,0:T(8,128)(2,1)} %copy-done.12, bf16[64,8,3584]{2,1,0:T(8,128)(2,1)} %all-to-all-done.own_down, ...), custom_call_target="tpu_custom_call" | custom-call | flops 16911433728 | bytes 55050240 | tf_op jit(solution)/shard_map/restore_and_run/pallas_call | solution.py:157
  274.9 11.2 %all-to-all-done.3.x_ref = bf16[64,8,3584]{2,1,0:T(8,128)(2,1)} async-done(((bf16[64,8,3584]{2,1,0:T(8,128)(2,1)}), bf16[64,8,3584]{2,1,0:T(8,128)(2,1)}, u32[]{:S(2)}, u32[]{:S(2)}) %all-to-all-start.3) | async-done | bytes 3670048 | tf_op jit(solution)/shard_map/all_to_all | solution.py:335
  286.1 18.3 %run_expert.1 = bf16[64,8,8960]{2,1,0:T(8,128)(2,1)} custom-call(bf16[64,8,3584]{2,1,0:T(8,128)(2,1)} %all-to-all-done.3.x_ref, bf16[3584,2048]{1,0:T(8,128)(2,1)} %get-tuple-element.37.gu_hbm, bf16[1024,3584]{1,0:T(8,128)(2,1)} %get-tuple-element.38.down_hbm, bf16[64,8,8960]{2,1,0:T(8,128)(2,1)} %get-tuple-element.39.produced), custom_call_target="tpu_custom_call", output_to_operand_aliasing={{}: (3, {})} | custom-call | flops 11274289152 | bytes 29360128 | tf_op jit(solution)/shard_map/run_expert/pallas_call | solution.py:225
  304.5 0.0 copy-start.2
  304.5 0.0 copy-start.1
  304.5 118.1 %all_to_all.27.x_ref = bf16[64,8,8960]{2,1,0:T(8,128)(2,1)S(1)} all-to-all(bf16[64,8,8960]{2,1,0:T(8,128)(2,1)} %run_expert.1), channel_id=1, replica_groups={{0,2,4,6,8,10,12,14,16,18,20,22,24,26,28,30,32,34,36,38,40,42,44,46,48,..., dimensions={0} | all-to-all | bytes 18350080 | tf_op jit(solution)/shard_map/all_to_all | solution.py:335
  422.6 0.0 copy-done.2
  422.6 7.7 %combine.1 = (bf16[128,3584]{1,0:T(8,128)(2,1)}, f32[64,128]{1,0:T(8,128)S(1)}) custom-call(bf16[64,8,8960]{2,1,0:T(8,128)(2,1)S(1)} %all_to_all.27.x_ref, s32[64,128]{1,0:T(8,128)S(1)} %fusion.3.rank_ref, f32[64,128]{1,0:T(8,128)S(1)} %select_reduce_fusion.1.gate_ref, bf16[128,3584]{1,0:T(8,128)(2,1)S(1)} %copy-done.2), custom_call_target="tpu_custom_call" | custom-call | flops 2818572288 | bytes 11010048 | tf_op jit(solution)/shard_map/combine/pallas_call | solution.py:293
  430.2 0.6 select_reduce_fusion
  430.9 0.0 copy-done.1
  (13 shorter events, 0.1 us)
Async XLA Ops:
  0.6 34.2 %copy-start = (bf16[128,3584]{1,0:T(8,128)(2,1)S(1)}, bf16[128,3584]{1,0:T(8,128)(2,1)}, u32[]{:S(2)}) copy-start(bf16[128,3584]{1,0:T(8,128)(2,1)} %param.9) | copy-start | bytes 2752516
  0.6 12.0 %copy-start.10 = (bf16[128,8]{0,1:T(8,128)(2,1)S(1)}, bf16[128,8]{0,1:T(8,128)(2,1)}, u32[]{:S(2)}) copy-start(bf16[128,8]{0,1:T(8,128)(2,1)} %param.12) | copy-start | bytes 6148
  0.7 12.0 %copy-start.11 = (s32[64]{0:T(128)S(1)}, s32[64]{0:T(128)}, u32[]{:S(2)}) copy-start(s32[64]{0:T(128)} %param.13) | copy-start | bytes 772
  0.7 12.0 %copy-start.9 = (s32[128,8]{0,1:T(8,128)S(1)}, s32[128,8]{0,1:T(8,128)}, u32[]{:S(2)}) copy-start(s32[128,8]{0,1:T(8,128)} %param.11) | copy-start | bytes 12292
  0.7 12.7 %copy-start.8 = (f32[64,8,28]{0,1,2:T(8,128)S(1)}, f32[64,8,28]{0,1,2:T(8,128)}, u32[]{:S(2)}) copy-start(f32[64,8,28]{0,1,2:T(8,128)} %param.17) | copy-start | bytes 172036
  0.7 13.0 %copy-start.7 = (f32[64,28,16]{0,2,1:T(8,128)S(1)}, f32[64,28,16]{0,2,1:T(8,128)}, u32[]{:S(2)}) copy-start(f32[64,28,16]{0,2,1:T(8,128)} %param.15) | copy-start | bytes 344068
  0.7 58.3 %all-to-all-start = ((bf16[64,8,3584]{2,1,0:T(8,128)(2,1)}), bf16[64,8,3584]{2,1,0:T(8,128)(2,1)}, u32[]{:S(2)}, u32[]{:S(2)}) async-start(bf16[64,8,3584]{2,1,0:T(8,128)(2,1)} %param.16), calls=%async_computation | async-start | bytes 7340032 | tf_op jit(solution)/shard_map/all_to_all | solution.py:335
  40.4 3.9 copy-start.4
  40.4 4.2 copy-start.5
  59.0 96.7 %copy-start.3 = (bf16[64,8,5376]{2,1,0:T(8,128)(2,1)S(1)}, bf16[64,8,5376]{2,1,0:T(8,128)(2,1)}, u32[]{:S(2)}) copy-start(bf16[64,8,5376]{2,1,0:T(8,128)(2,1)} %pad_maximum_fusion) | copy-start | bytes 16515076
  155.7 73.7 %copy-start.6 = (bf16[64,8,7168]{2,1,0:T(8,128)(2,1)}, bf16[64,8,7168]{2,1,0:T(8,128)(2,1)S(1)}, u32[]{:S(2)}) copy-start(bf16[64,8,7168]{2,1,0:T(8,128)(2,1)S(1)} %all_to_all.25.own_gu) | copy-start | bytes 22020100
  155.7 73.7 %collective-permute-start = (bf16[64,8,7168]{2,1,0:T(8,128)(2,1)S(1)}, bf16[64,8,7168]{2,1,0:T(8,128)(2,1)S(1)}, u32[]{:S(2)}, u32[]{:S(2)}) collective-permute-start(bf16[64,8,7168]{2,1,0:T(8,128)(2,1)S(1)} %all_to_all.25.own_gu), channel_id=1, source_target_pairs={{0,1},{1,0},{2,3},{3,2},{4,5},{5,4},{6,7},{7,6},{8,9},{9,8},{10,11... | collective-permute-start | bytes 22020104 | tf_op jit(solution)/shard_map/ppermute | solution.py:389
  229.4 2.9 copy-start.12
  232.3 6.8 %collective-permute-start.1 = (bf16[64,8,3584]{2,1,0:T(8,128)(2,1)}, bf16[64,8,3584]{2,1,0:T(8,128)(2,1)}, u32[]{:S(2)}, u32[]{:S(2)}) collective-permute-start(bf16[64,8,3584]{2,1,0:T(8,128)(2,1)} %all-to-all-done.own_down), channel_id=1, source_target_pairs={{0,1},{1,0},{2,3},{3,2},{4,5},{5,4},{6,7},{7,6},{8,9},{9,8},{10,11... | collective-permute-start | bytes 11010056 | tf_op jit(solution)/shard_map/ppermute | solution.py:395
  232.3 53.8 %all-to-all-start.3 = ((bf16[64,8,3584]{2,1,0:T(8,128)(2,1)}), bf16[64,8,3584]{2,1,0:T(8,128)(2,1)}, u32[]{:S(2)}, u32[]{:S(2)}) async-start(bf16[64,8,3584]{2,1,0:T(8,128)(2,1)} %fusion), calls=%async_computation.3 | async-start | bytes 7340032 | tf_op jit(solution)/shard_map/all_to_all | solution.py:335
  304.5 118.1 %copy-start.2 = (bf16[128,3584]{1,0:T(8,128)(2,1)S(1)}, bf16[128,3584]{1,0:T(8,128)(2,1)}, u32[]{:S(2)}) copy-start(bf16[128,3584]{1,0:T(8,128)(2,1)} %cotangent_ref.1) | copy-start | bytes 2752516
  304.5 126.4 %copy-start.1 = (bf16[128,3584]{1,0:T(8,128)(2,1)S(1)}, bf16[128,3584]{1,0:T(8,128)(2,1)}, u32[]{:S(2)}) copy-start(bf16[128,3584]{1,0:T(8,128)(2,1)} %param.9) | copy-start | bytes 2752516

commit v5 on v4

--- a/solution.py
+++ b/solution.py
@@ -48,21 +48,21 @@
         down_ref[pl.ds(start, 16), :] = jnp.concatenate(both, axis=0).astype(jnp.bfloat16)
 
 
-def expert_rows(place, x_ref, out_ref, gu_ref, down_ref, rows_ref, active_ref, ready):
-    peers, _, packed = x_ref.shape
+def expert_rows(place, parts, out_ref, gu_ref, down_ref, rows_ref, active_ref, ready):
+    peers = parts[0].shape[0]
     width = rows_ref.shape[1]
     half = width // 2
-    full = packed // width
+    full, folded = len(parts) // 2, len(parts) % 2 == 1
     eight = 8 * peers
     chunks = FF // COLS
 
     for q in range(0, peers, 4):
-        for g in range(full):
-            rows_ref[pl.ds(g * eight + 8 * q, 32), :] = in_rows(
-                x_ref[q : q + 4, :, g * width : (g + 1) * width]
+        for g in range(2 * full):
+            rows_ref[pl.ds(g // 2 * eight + 8 * q, 32), pl.ds(g % 2 * half, half)] = in_rows(
+                parts[g][q : q + 4]
             )
-        if packed > full * width:
-            fold = [x_ref[p, :, full * width :].astype(jnp.float32) for p in range(q, q + 4)]
+        if folded:
+            fold = [parts[-1][p].astype(jnp.float32) for p in range(q, q + 4)]
             for part, first in ((0, 0), (1, 4)):
                 rows_ref[pl.ds(full * eight + 4 * q, 16), pl.ds(part * half, half)] = (
                     jnp.concatenate([f[first : first + 4] for f in fold], axis=0)
@@ -96,7 +96,7 @@
                 out_ref[:, :, to : to + COLS] = (
                     y[g * eight : (g + 1) * eight].reshape(peers, 8, COLS).astype(jnp.bfloat16)
                 )
-        if packed > full * width:
+        if folded:
             for p in range(peers):
                 at = full * eight + 4 * p
                 to = place + full * width + j * COLS
@@ -105,7 +105,7 @@
                 ).astype(jnp.bfloat16)
 
 
-def first_kernel(place, parity_ref, own_gu, other_gu, own_down, other_down, gu_scale_ref, down_scale_ref, x_ref, out_ref, gu_hbm, down_hbm, gu_ref, down_ref, rows_ref, active_ref, sems):
+def first_kernel(place, parity_ref, own_gu, other_gu, own_down, other_down, gu_scale_ref, down_scale_ref, x_a, x_b, x_c, out_ref, gu_hbm, down_hbm, gu_ref, down_ref, rows_ref, active_ref, sems):
     step = pl.program_id(0)
     restoring = gu_ref.shape[0] // (56 * own_gu.shape[0])
     scales = (gu_scale_ref, down_scale_ref)
@@ -130,7 +130,9 @@
 
     @pl.when(step >= restoring)
     def _():
-        expert_rows(place, x_ref, out_ref, gu_ref, down_ref, rows_ref, active_ref, lambda j: None)
+        expert_rows(
+            place, (x_a, x_b, x_c), out_ref, gu_ref, down_ref, rows_ref, active_ref, lambda j: None
+        )
 
     @pl.when(step == pl.num_programs(0) - 1)
     def _():
@@ -138,10 +140,10 @@
             copy.wait()
 
 
-def run_first(arrived, own_gu, other_gu, own_down, other_down, gu_scale, down_scale, parity, place):
-    peers, _, packed = arrived.shape
+def run_first(own, other_gu, own_down, other_down, gu_scale, down_scale, parity, place):
+    peers, _, packed = other_gu.shape
     width = down_scale.shape[1]
-    each = 8 * packed // width
+    each = 12
     total = width * 5 // 2
     group, chips = 32, 4
     restoring = peers // chips
@@ -150,8 +152,10 @@
     def part(count):
         return pl.BlockSpec((chips, 8, count), lambda i: (jnp.minimum(i, restoring - 1), 0, 0))
 
-    def piece(count):
-        return pl.BlockSpec((group, 8, count), lambda i: (jnp.maximum(i - restoring, 0), 0, 0))
+    def piece(count, at=0):
+        return pl.BlockSpec((group, 8, count), lambda i: (jnp.maximum(i - restoring, 0), 0, at))
+
+    after = 2 * packed // width
 
     gu_shape, down_shape = (width, 2 * FF), (FF, width)
     return pl.pallas_call(
@@ -159,14 +163,14 @@
         grid=(restoring + peers // group,),
         in_specs=[
             pl.BlockSpec(memory_space=pltpu.SMEM),
-            part(own_gu.shape[2]),
-            part(own_gu.shape[2]),
+            part(packed),
+            part(packed),
             part(width),
             part(width),
             pl.BlockSpec(gu_scale.shape, lambda i: (0, 0)),
             pl.BlockSpec(down_scale.shape, lambda i: (0, 0)),
-            piece(packed),
-        ],
+        ]
+        + [piece(width // 2, after + k) for k in range(3)],
         out_specs=[piece(total), pl.BlockSpec(memory_space=pl.ANY), pl.BlockSpec(memory_space=pl.ANY)],
         out_shape=[
             jax.ShapeDtypeStruct((peers, 8, total), jnp.bfloat16),
@@ -187,10 +191,10 @@
             transcendentals=rows * FF,
         ),
         name="restore_and_run",
-    )(parity, own_gu, other_gu, own_down, other_down, gu_scale, down_scale, arrived)
-
-
-def expert_kernel(x_ref, gu_hbm, down_hbm, produced, out_ref, gu_ref, down_ref, rows_ref, active_ref, sems):
+    )(parity, own, other_gu, own_down, other_down, gu_scale, down_scale, own, own, own)
+
+
+def expert_kernel(x_a, x_b, gu_hbm, down_hbm, produced, out_ref, gu_ref, down_ref, rows_ref, active_ref, sems):
     step = pl.program_id(0)
     copies = []
     for j in range(FF // COLS):
@@ -212,7 +216,7 @@
             for copy in copies[2 * j : 2 * j + 2]:
                 copy.wait()
 
-    expert_rows(0, x_ref, out_ref, gu_ref, down_ref, rows_ref, active_ref, ready)
+    expert_rows(0, (x_a, x_b), out_ref, gu_ref, down_ref, rows_ref, active_ref, ready)
 
 
 def run_expert(arrived, w_gu, w_down, produced):
@@ -222,13 +226,14 @@
     group = 64
     rows = peers * each
     piece = pl.BlockSpec((group, 8, packed), lambda i: (i, 0, 0))
+    halves = [pl.BlockSpec((group, 8, packed // 2), lambda i, at=at: (i, 0, at)) for at in range(2)]
     return pl.pallas_call(
         expert_kernel,
         grid=(peers // group,),
-        in_specs=[piece] + [pl.BlockSpec(memory_space=pl.ANY)] * 3,
+        in_specs=halves + [pl.BlockSpec(memory_space=pl.ANY)] * 3,
         out_specs=piece,
         out_shape=jax.ShapeDtypeStruct(produced.shape, jnp.bfloat16),
-        input_output_aliases={3: 0},
+        input_output_aliases={4: 0},
         scratch_shapes=[
             pltpu.VMEM(w_gu.shape, jnp.bfloat16),
             pltpu.VMEM(w_down.shape, jnp.bfloat16),
@@ -243,7 +248,7 @@
             transcendentals=rows * FF,
         ),
         name="run_expert",
-    )(arrived, w_gu, w_down, produced)
+    )(arrived, arrived, w_gu, w_down, produced)
 
 
 def combine_kernel(x_ref, rank_ref, gate_ref, cotangent_ref, out_ref, grad_ref, sum_ref):
@@ -335,19 +340,12 @@
         return lax.all_to_all(x, "expert", 0, 0, axis_index_groups=same_core, tiled=True)
 
     down_own = exchange(down_payload)
-    packed = jnp.concatenate(
-        [lax.dynamic_slice_in_dim(gu_payload, 4 * core + 8 * g, 8, axis=1) for g in range(3)]
-        + [
-            jnp.concatenate(
-                [
-                    lax.dynamic_slice_in_dim(gu_payload[:, :, half_ff : half_ff + FF], 24 - 24 * core, 4, axis=1)
-                    for half_ff in (0, FF)
-                ],
-                axis=1,
-            )
-        ],
-        axis=2,
-    )
+    gu_parts = [lax.dynamic_slice_in_dim(gu_payload, 4 * core + 8 * g, 8, axis=1) for g in range(3)]
+    gu_fold = [
+        lax.dynamic_slice_in_dim(gu_payload[:, :, at : at + FF], 24 - 24 * core, 4, axis=1)
+        for at in (0, FF)
+    ]
+    gu_parts.append(jnp.concatenate(gu_fold, axis=1))
     gu_scale = jnp.repeat(gu_scales[chip], 128, axis=1)
     down_scale = jnp.repeat(down_scales[chip], 128, axis=1)
 
@@ -377,24 +375,19 @@
     outgoing_a = picked(eight)
     last = picked(16 + eight % 4)
     last = jnp.where(eight[None, :, None] < 4, last[:, :, :half], last[:, :, half:])
-    outgoing_b = jnp.concatenate([picked(8 + eight), last], axis=2)
-
-    packed, outgoing_a, outgoing_b, down_own, rank, gate_of, gu_scale, down_scale = (
-        lax.optimization_barrier(
-            (packed, outgoing_a, outgoing_b, down_own, rank, gate_of, gu_scale, down_scale)
-        )
+    packed = jnp.concatenate(gu_parts + [picked(8 + eight), last], axis=2)
+    gu_width = 7 * FF
+
+    packed, outgoing_a, down_own, rank, gate_of, gu_scale, down_scale = lax.optimization_barrier(
+        (packed, outgoing_a, down_own, rank, gate_of, gu_scale, down_scale)
     )
-    gu_own = exchange(packed)
-    gu_own, outgoing_b = lax.optimization_barrier((gu_own, outgoing_b))
-    gu_other = lax.ppermute(gu_own, "expert", swap)
-    arrived_b = exchange(outgoing_b)
-    arrived_b, gu_other, down_own, outgoing_a = lax.optimization_barrier(
-        (arrived_b, gu_other, down_own, outgoing_a)
-    )
+    own = exchange(packed)
+    own, down_own, outgoing_a = lax.optimization_barrier((own, down_own, outgoing_a))
     arrived_a = exchange(outgoing_a)
     down_other = lax.ppermute(down_own, "expert", swap)
+    gu_other = lax.ppermute(own[:, :, :gu_width], "expert", swap)
     produced, w_gu, w_down = run_first(
-        arrived_b, gu_own, gu_other, down_own, down_other, gu_scale, down_scale, parity, model_width
+        own, gu_other, down_own, down_other, gu_scale, down_scale, parity, model_width
     )
     produced, arrived_a = lax.optimization_barrier((produced, arrived_a))
     produced = run_expert(arrived_a, w_gu, w_down, produced)

time: 432 us -> 420 us (0.972)
  blocking collectives: 288 us -> 272 us
  local copies, waits for them, and re-layouts: 25.7 us -> 30.6 us
    all_to_all x3 -> x2, blocking collectives: 288 us -> 272 us  [exchange(): lax.all_to_all(x, 'expert', 0, 0, axis_index_groups=same_core, tiled=True)]
    all_to_all x2, waiting for transfers between devices: 21.7 us -> 13.7 us  [exchange(): lax.all_to_all(x, 'expert', 0, 0, axis_index_groups=same_core, tiled=True)]
    ppermute x1, waiting for transfers between devices: 0.28 us -> 8.16 us  [shards(): down_other = lax.ppermute(down_own, 'expert', swap)]
    slice x1 -> x2, local copies, waits for them, and re-layouts: 7.62 us -> 14.1 us  [the longest x1 7.63 us: shards(): gu_payload[:, :, at:at + FF]]
    concatenate x2 -> x1, other arithmetic: 7.11 us -> 1.88 us  [shards(): packed = jnp.concatenate(gu_parts + [picked(8 + eight), last], axis=2)]
    unnamed x33 -> x23, local copies, waits for them, and re-layouts: 11 us -> 9.3 us
  transfers between devices with their start and end apart: 4 -> 4, of which waited for: 3 -> 3; matrix products, arithmetic and copies ran while one was open for 8% -> 8% of each run, Pallas kernels for 8% -> 9%
where the time goes in v5:
time: 420 us
  blocking collectives  272 us (65%)
  Pallas kernels  61.8 us (15%)
  local copies, waits for them, and re-layouts  30.6 us (7%)
  waiting for transfers between devices  21.9 us (5%)
  starting transfers between devices  21 us (5%)
  matrix products  7.29 us (2%)
  other arithmetic  4.22 us (1%)
    all_to_all x2, blocking collectives, exchange(): lax.all_to_all(x, 'expert', 0, 0, axis_index_groups=same_core, tiled=True)  272 us
    pallas_call x1, Pallas kernels, run_first(): pl.pallas_call(functools.partial(first_kernel, place), grid=(restoring +...  35.8 us
    all_to_all x2, starting transfers between devices, exchange(): lax.all_to_all(x, 'expert', 0, 0, axis_index_groups=same_core, tiled=True)  20.4 us
    pallas_call x1, Pallas kernels, run_expert(): pl.pallas_call(expert_kernel, grid=(peers // group,), in_specs=halves + [...  18.3 us
    all_to_all x2, waiting for transfers between devices, exchange(): lax.all_to_all(x, 'expert', 0, 0, axis_index_groups=same_core, tiled=True)  13.7 us
    unnamed x23, local copies, waits for them, and re-layouts  9.3 us
  transfers between devices with their start and end apart: 4, of which 3 were waited for; matrix products, arithmetic and copies ran while one was open for 8% of the time, Pallas kernels for 9%

profile of v5, /device:TPU:0, one launch (start us, length us, event | category | flops | bytes accessed | tf_op | source)
XLA Modules:
  0.0 419.7 jit_solution(10206742182308162506)
XLA Ops:
  0.6 0.0 copy-start
  0.6 0.0 copy-start.6
  0.7 0.0 copy-start.7
  0.7 0.0 copy-start.5
  0.7 0.0 copy-start.4
  0.7 0.0 copy-start.3
  0.7 11.9 %all-to-all-start = ((bf16[64,8,3584]{2,1,0:T(8,128)(2,1)}), bf16[64,8,3584]{2,1,0:T(8,128)(2,1)}, u32[]{:S(2)}, u32[]{:S(2)}) async-start(bf16[64,8,3584]{2,1,0:T(8,128)(2,1)} %param.16), calls=%async_computation | async-start | bytes 7340032 | tf_op jit(solution)/shard_map/all_to_all | solution.py:340
  12.7 0.0 copy-done.6
  12.7 0.0 copy-done.7
  12.7 0.0 copy-done.5
  12.7 0.1 select_reduce_fusion.2
  12.9 0.1 eq.95
  13.0 0.1 eq.91
  13.1 0.1 eq.99
  13.2 0.0 copy-done.4
  13.2 0.1 constant_dynamic-slice_fusion.1
  13.3 0.2 copy.45
  13.6 0.0 copy-done.3
  13.6 0.1 constant_dynamic-slice_fusion
  13.7 0.2 copy.44
  13.9 0.1 broadcast_in_dim.73
  14.1 0.8 copy.46
  14.9 7.6 %fusion.14 = (bf16[64,28,1024]{2,0,1:T(8,128)(2,1)}, bf16[64,28,1024]{2,0,1:T(8,128)(2,1)}) fusion(bf16[64,28,2048]{2,0,1:T(8,128)(2,1)} %param.14), kind=kLoop, calls=%fused_computation.44 | loop fusion | bytes 14680064 | tf_op jit(solution)/shard_map/slice | solution.py:345
  22.5 1.3 constant_dynamic-slice_fusion.2
  23.8 0.4 copy.41
  24.3 0.4 copy.39
  24.7 4.0 constant_dynamic-slice_fusion.4
  28.7 2.6 copy_dynamic-update-slice_fusion.2
  31.3 2.5 copy_dynamic-update-slice_fusion.1
  33.8 2.5 copy_dynamic-update-slice_fusion
  36.3 1.5 maximum_dynamic-update-slice_fusion
  37.8 0.1 fusion.5.rank_ref
  38.0 0.0 copy-done
  38.0 3.0 fusion.3
  40.9 1.2 fusion.2
  42.1 3.0 fusion.1
  45.1 1.9 fusion.4
  47.0 0.7 broadcast_bitcast_fusion.down_scale_ref
  47.7 11.3 %all-to-all-done.own_down = bf16[64,8,3584]{2,1,0:T(8,128)(2,1)} async-done(((bf16[64,8,3584]{2,1,0:T(8,128)(2,1)}), bf16[64,8,3584]{2,1,0:T(8,128)(2,1)}, u32[]{:S(2)}, u32[]{:S(2)}) %all-to-all-start) | async-done | bytes 3670048 | tf_op jit(solution)/shard_map/all_to_all | solution.py:340
  59.0 156.0 %all_to_all.20.own_gu.x_a.x_b.x_c = bf16[64,8,12544]{2,1,0:T(8,128)(2,1)} all-to-all(bf16[64,8,12544]{2,1,0:T(8,128)(2,1)} %fusion.4), channel_id=1, replica_groups={{0,2,4,6,8,10,12,14,16,18,20,22,24,26,28,30,32,34,36,38,40,42,44,46,48,..., dimensions={0} | all-to-all | bytes 25690112 | tf_op jit(solution)/shard_map/all_to_all | solution.py:340
  215.0 6.5 %slice.19 = bf16[64,8,7168]{2,1,0:T(8,128)(2,1)} slice(bf16[64,8,12544]{2,1,0:T(8,128)(2,1)} %all_to_all.20.own_gu.x_a.x_b.x_c), slice={[0:64], [0:8], [0:7168]} | slice | bytes 14680064 | tf_op jit(solution)/shard_map/slice | solution.py:388
  221.5 0.0 collective-permute-start
  221.5 0.5 collective-permute-start.1
  222.0 8.6 %all-to-all-start.2 = ((bf16[64,8,3584]{2,1,0:T(8,128)(2,1)}), bf16[64,8,3584]{2,1,0:T(8,128)(2,1)}, u32[]{:S(2)}, u32[]{:S(2)}) async-start(bf16[64,8,3584]{2,1,0:T(8,128)(2,1)} %fusion.3), calls=%async_computation.2 | async-start | bytes 7340032 | tf_op jit(solution)/shard_map/all_to_all | solution.py:340
  230.6 8.2 %collective-permute-done.1.other_down = bf16[64,8,3584]{2,1,0:T(8,128)(2,1)} collective-permute-done((bf16[64,8,3584]{2,1,0:T(8,128)(2,1)}, bf16[64,8,3584]{2,1,0:T(8,128)(2,1)}, u32[]{:S(2)}, u32[]{:S(2)}) %collective-permute-start.1) | collective-permute-done | bytes 3670048 | tf_op jit(solution)/shard_map/ppermute | solution.py:387
  238.7 0.0 collective-permute-done.other_gu
  238.7 35.8 %restore_and_run.1 = (bf16[64,8,8960]{2,1,0:T(8,128)(2,1)}, bf16[3584,2048]{1,0:T(8,128)(2,1)}, bf16[1024,3584]{1,0:T(8,128)(2,1)}) custom-call(s32[1]{0:T(128)} %bitcast.parity_ref, bf16[64,8,12544]{2,1,0:T(8,128)(2,1)} %all_to_all.20.own_gu.x_a.x_b.x_c, bf16[64,8,7168]{2,1,0:T(8,128)(2,1)} %collective-permute-done.other_gu, ...), custom_call_target="tpu_custom_call" | custom-call | flops 16911433728 | bytes 55050240 | tf_op jit(solution)/shard_map/restore_and_run/pallas_call | solution.py:161
  274.5 2.5 all-to-all-done.2.x_a.x_b
  277.0 18.3 %run_expert.1 = bf16[64,8,8960]{2,1,0:T(8,128)(2,1)} custom-call(bf16[64,8,3584]{2,1,0:T(8,128)(2,1)} %all-to-all-done.2.x_a.x_b, bf16[64,8,3584]{2,1,0:T(8,128)(2,1)} %all-to-all-done.2.x_a.x_b, bf16[3584,2048]{1,0:T(8,128)(2,1)} %get-tuple-element.29.gu_hbm, bf16[1024,3584]{1,0:T(8,128)(2,1)} %get-tuple-element.30.down_hbm, ...), custom_call_target="tpu_custom_call", output_to_operand_aliasing={{}: (4, {})} | custom-call | flops 11274289152 | bytes 29360128 | tf_op jit(solution)/shard_map/run_expert/pallas_call | solution.py:230
  295.3 0.0 copy-start.2
  295.3 0.0 copy-start.1
  295.4 116.0 %all_to_all.21.x_ref = bf16[64,8,8960]{2,1,0:T(8,128)(2,1)S(1)} all-to-all(bf16[64,8,8960]{2,1,0:T(8,128)(2,1)} %run_expert.1), channel_id=1, replica_groups={{0,2,4,6,8,10,12,14,16,18,20,22,24,26,28,30,32,34,36,38,40,42,44,46,48,..., dimensions={0} | all-to-all | bytes 18350080 | tf_op jit(solution)/shard_map/all_to_all | solution.py:340
  411.4 0.0 copy-done.2
  411.4 7.7 %combine.1 = (bf16[128,3584]{1,0:T(8,128)(2,1)}, f32[64,128]{1,0:T(8,128)S(1)}) custom-call(bf16[64,8,8960]{2,1,0:T(8,128)(2,1)S(1)} %all_to_all.21.x_ref, s32[64,128]{1,0:T(8,128)S(1)} %fusion.5.rank_ref, f32[64,128]{1,0:T(8,128)S(1)} %select_reduce_fusion.1.gate_ref, bf16[128,3584]{1,0:T(8,128)(2,1)S(1)} %copy-done.2), custom_call_target="tpu_custom_call" | custom-call | flops 2818572288 | bytes 11010048 | tf_op jit(solution)/shard_map/combine/pallas_call | solution.py:298
  419.1 0.6 select_reduce_fusion
  419.7 0.0 copy-done.1
  (10 shorter events, 0.1 us)
Async XLA Ops:
  0.6 37.3 %copy-start = (bf16[128,3584]{1,0:T(8,128)(2,1)S(1)}, bf16[128,3584]{1,0:T(8,128)(2,1)}, u32[]{:S(2)}) copy-start(bf16[128,3584]{1,0:T(8,128)(2,1)} %param.9) | copy-start | bytes 2752516
  0.6 12.0 %copy-start.6 = (bf16[128,8]{0,1:T(8,128)(2,1)S(1)}, bf16[128,8]{0,1:T(8,128)(2,1)}, u32[]{:S(2)}) copy-start(bf16[128,8]{0,1:T(8,128)(2,1)} %param.12) | copy-start | bytes 6148
  0.7 12.0 %copy-start.7 = (s32[64]{0:T(128)S(1)}, s32[64]{0:T(128)}, u32[]{:S(2)}) copy-start(s32[64]{0:T(128)} %param.13) | copy-start | bytes 772
  0.7 12.0 %copy-start.5 = (s32[128,8]{0,1:T(8,128)S(1)}, s32[128,8]{0,1:T(8,128)}, u32[]{:S(2)}) copy-start(s32[128,8]{0,1:T(8,128)} %param.11) | copy-start | bytes 12292
  0.7 12.5 %copy-start.4 = (f32[64,8,28]{0,1,2:T(8,128)S(1)}, f32[64,8,28]{0,1,2:T(8,128)}, u32[]{:S(2)}) copy-start(f32[64,8,28]{0,1,2:T(8,128)} %param.17) | copy-start | bytes 172036
  0.7 12.9 %copy-start.3 = (f32[64,28,16]{0,2,1:T(8,128)S(1)}, f32[64,28,16]{0,2,1:T(8,128)}, u32[]{:S(2)}) copy-start(f32[64,28,16]{0,2,1:T(8,128)} %param.15) | copy-start | bytes 344068
  0.7 58.3 %all-to-all-start = ((bf16[64,8,3584]{2,1,0:T(8,128)(2,1)}), bf16[64,8,3584]{2,1,0:T(8,128)(2,1)}, u32[]{:S(2)}, u32[]{:S(2)}) async-start(bf16[64,8,3584]{2,1,0:T(8,128)(2,1)} %param.16), calls=%async_computation | async-start | bytes 7340032 | tf_op jit(solution)/shard_map/all_to_all | solution.py:340
  221.5 17.3 %collective-permute-start = (bf16[64,8,7168]{2,1,0:T(8,128)(2,1)}, bf16[64,8,7168]{2,1,0:T(8,128)(2,1)}, u32[]{:S(2)}, u32[]{:S(2)}) collective-permute-start(bf16[64,8,7168]{2,1,0:T(8,128)(2,1)} %slice.19), channel_id=1, source_target_pairs={{0,1},{1,0},{2,3},{3,2},{4,5},{5,4},{6,7},{7,6},{8,9},{9,8},{10,11... | collective-permute-start | bytes 22020104 | tf_op jit(solution)/shard_map/ppermute | solution.py:388
  221.5 17.2 %collective-permute-start.1 = (bf16[64,8,3584]{2,1,0:T(8,128)(2,1)}, bf16[64,8,3584]{2,1,0:T(8,128)(2,1)}, u32[]{:S(2)}, u32[]{:S(2)}) collective-permute-start(bf16[64,8,3584]{2,1,0:T(8,128)(2,1)} %all-to-all-done.own_down), channel_id=1, source_target_pairs={{0,1},{1,0},{2,3},{3,2},{4,5},{5,4},{6,7},{7,6},{8,9},{9,8},{10,11... | collective-permute-start | bytes 11010056 | tf_op jit(solution)/shard_map/ppermute | solution.py:387
  222.0 55.0 %all-to-all-start.2 = ((bf16[64,8,3584]{2,1,0:T(8,128)(2,1)}), bf16[64,8,3584]{2,1,0:T(8,128)(2,1)}, u32[]{:S(2)}, u32[]{:S(2)}) async-start(bf16[64,8,3584]{2,1,0:T(8,128)(2,1)} %fusion.3), calls=%async_computation.2 | async-start | bytes 7340032 | tf_op jit(solution)/shard_map/all_to_all | solution.py:340
  295.3 116.0 %copy-start.2 = (bf16[128,3584]{1,0:T(8,128)(2,1)S(1)}, bf16[128,3584]{1,0:T(8,128)(2,1)}, u32[]{:S(2)}) copy-start(bf16[128,3584]{1,0:T(8,128)(2,1)} %cotangent_ref.1) | copy-start | bytes 2752516
  295.3 124.3 %copy-start.1 = (bf16[128,3584]{1,0:T(8,128)(2,1)S(1)}, bf16[128,3584]{1,0:T(8,128)(2,1)}, u32[]{:S(2)}) copy-start(bf16[128,3584]{1,0:T(8,128)(2,1)} %param.9) | copy-start | bytes 2752516

commit v6 on v5

--- a/solution.py
+++ b/solution.py
@@ -10,7 +10,7 @@
 FF = 1024
 TOP = 8
 COLS = 256
-GROUP = 16
+GROUP = 32
 
 
 def in_rows(block):

time: 420 us -> 419 us (level)
  no operation moved by 1% of the time
where the time goes in v6:
time: 419 us; the launch traced here: 418 us
  blocking collectives  272 us (65%)
  Pallas kernels  60 us (14%)
  local copies, waits for them, and re-layouts  30.6 us (7%)
  waiting for transfers between devices  21.9 us (5%)
  starting transfers between devices  21 us (5%)
  matrix products  7.29 us (2%)
  other arithmetic  4.22 us (1%)
    all_to_all x2, blocking collectives, exchange(): lax.all_to_all(x, 'expert', 0, 0, axis_index_groups=same_core, tiled=True)  272 us
    pallas_call x1, Pallas kernels, run_first(): pl.pallas_call(functools.partial(first_kernel, place), grid=(restoring +...  35.8 us
    all_to_all x2, starting transfers between devices, exchange(): lax.all_to_all(x, 'expert', 0, 0, axis_index_groups=same_core, tiled=True)  20.4 us
    pallas_call x1, Pallas kernels, run_expert(): pl.pallas_call(expert_kernel, grid=(peers // group,), in_specs=halves + [...  18.3 us
    all_to_all x2, waiting for transfers between devices, exchange(): lax.all_to_all(x, 'expert', 0, 0, axis_index_groups=same_core, tiled=True)  13.7 us
    unnamed x23, local copies, waits for them, and re-layouts  9.3 us
  transfers between devices with their start and end apart: 4, of which 3 were waited for; matrix products, arithmetic and copies ran while one was open for 8% of the time, Pallas kernels for 9%

profile of v6, /device:TPU:0, one launch (start us, length us, event | category | flops | bytes accessed | tf_op | source)
XLA Modules:
  0.0 417.9 jit_solution(15768421618050709502)
XLA Ops:
  0.6 0.0 copy-start
  0.6 0.0 copy-start.6
  0.7 0.0 copy-start.7
  0.7 0.0 copy-start.5
  0.7 0.0 copy-start.4
  0.7 0.0 copy-start.3
  0.7 11.9 %all-to-all-start = ((bf16[64,8,3584]{2,1,0:T(8,128)(2,1)}), bf16[64,8,3584]{2,1,0:T(8,128)(2,1)}, u32[]{:S(2)}, u32[]{:S(2)}) async-start(bf16[64,8,3584]{2,1,0:T(8,128)(2,1)} %param.16), calls=%async_computation | async-start | bytes 7340032 | tf_op jit(solution)/shard_map/all_to_all | solution.py:340
  12.7 0.0 copy-done.6
  12.7 0.0 copy-done.7
  12.7 0.0 copy-done.5
  12.7 0.1 select_reduce_fusion.2
  12.9 0.1 eq.95
  13.0 0.1 eq.91
  13.1 0.1 eq.99
  13.2 0.0 copy-done.4
  13.2 0.1 constant_dynamic-slice_fusion.1
  13.3 0.2 copy.45
  13.6 0.0 copy-done.3
  13.6 0.1 constant_dynamic-slice_fusion
  13.7 0.2 copy.44
  13.9 0.1 broadcast_in_dim.73
  14.1 0.8 copy.46
  14.9 7.6 %fusion.14 = (bf16[64,28,1024]{2,0,1:T(8,128)(2,1)}, bf16[64,28,1024]{2,0,1:T(8,128)(2,1)}) fusion(bf16[64,28,2048]{2,0,1:T(8,128)(2,1)} %param.14), kind=kLoop, calls=%fused_computation.44 | loop fusion | bytes 14680064 | tf_op jit(solution)/shard_map/slice | solution.py:345
  22.5 1.3 constant_dynamic-slice_fusion.2
  23.8 0.4 copy.41
  24.3 0.4 copy.39
  24.7 4.0 constant_dynamic-slice_fusion.4
  28.7 2.6 copy_dynamic-update-slice_fusion.2
  31.3 2.5 copy_dynamic-update-slice_fusion.1
  33.8 2.5 copy_dynamic-update-slice_fusion
  36.3 1.5 maximum_dynamic-update-slice_fusion
  37.8 0.1 fusion.5.rank_ref
  38.0 0.0 copy-done
  38.0 3.0 fusion.3
  40.9 1.2 fusion.2
  42.1 3.0 fusion.1
  45.1 1.9 fusion.4
  47.0 0.7 broadcast_bitcast_fusion.down_scale_ref
  47.7 11.3 %all-to-all-done.own_down = bf16[64,8,3584]{2,1,0:T(8,128)(2,1)} async-done(((bf16[64,8,3584]{2,1,0:T(8,128)(2,1)}), bf16[64,8,3584]{2,1,0:T(8,128)(2,1)}, u32[]{:S(2)}, u32[]{:S(2)}) %all-to-all-start) | async-done | bytes 3670048 | tf_op jit(solution)/shard_map/all_to_all | solution.py:340
  59.0 156.0 %all_to_all.20.own_gu.x_a.x_b.x_c = bf16[64,8,12544]{2,1,0:T(8,128)(2,1)} all-to-all(bf16[64,8,12544]{2,1,0:T(8,128)(2,1)} %fusion.4), channel_id=1, replica_groups={{0,2,4,6,8,10,12,14,16,18,20,22,24,26,28,30,32,34,36,38,40,42,44,46,48,..., dimensions={0} | all-to-all | bytes 25690112 | tf_op jit(solution)/shard_map/all_to_all | solution.py:340
  215.0 6.5 %slice.19 = bf16[64,8,7168]{2,1,0:T(8,128)(2,1)} slice(bf16[64,8,12544]{2,1,0:T(8,128)(2,1)} %all_to_all.20.own_gu.x_a.x_b.x_c), slice={[0:64], [0:8], [0:7168]} | slice | bytes 14680064 | tf_op jit(solution)/shard_map/slice | solution.py:388
  221.5 0.0 collective-permute-start
  221.5 0.5 collective-permute-start.1
  222.0 8.6 %all-to-all-start.2 = ((bf16[64,8,3584]{2,1,0:T(8,128)(2,1)}), bf16[64,8,3584]{2,1,0:T(8,128)(2,1)}, u32[]{:S(2)}, u32[]{:S(2)}) async-start(bf16[64,8,3584]{2,1,0:T(8,128)(2,1)} %fusion.3), calls=%async_computation.2 | async-start | bytes 7340032 | tf_op jit(solution)/shard_map/all_to_all | solution.py:340
  230.6 8.2 %collective-permute-done.1.other_down = bf16[64,8,3584]{2,1,0:T(8,128)(2,1)} collective-permute-done((bf16[64,8,3584]{2,1,0:T(8,128)(2,1)}, bf16[64,8,3584]{2,1,0:T(8,128)(2,1)}, u32[]{:S(2)}, u32[]{:S(2)}) %collective-permute-start.1) | collective-permute-done | bytes 3670048 | tf_op jit(solution)/shard_map/ppermute | solution.py:387
  238.7 0.0 collective-permute-done.other_gu
  238.7 35.8 %restore_and_run.1 = (bf16[64,8,8960]{2,1,0:T(8,128)(2,1)}, bf16[3584,2048]{1,0:T(8,128)(2,1)}, bf16[1024,3584]{1,0:T(8,128)(2,1)}) custom-call(s32[1]{0:T(128)} %bitcast.parity_ref, bf16[64,8,12544]{2,1,0:T(8,128)(2,1)} %all_to_all.20.own_gu.x_a.x_b.x_c, bf16[64,8,7168]{2,1,0:T(8,128)(2,1)} %collective-permute-done.other_gu, ...), custom_call_target="tpu_custom_call" | custom-call | flops 16911433728 | bytes 55050240 | tf_op jit(solution)/shard_map/restore_and_run/pallas_call | solution.py:161
  274.5 2.5 all-to-all-done.2.x_a.x_b
  277.0 18.3 %run_expert.1 = bf16[64,8,8960]{2,1,0:T(8,128)(2,1)} custom-call(bf16[64,8,3584]{2,1,0:T(8,128)(2,1)} %all-to-all-done.2.x_a.x_b, bf16[64,8,3584]{2,1,0:T(8,128)(2,1)} %all-to-all-done.2.x_a.x_b, bf16[3584,2048]{1,0:T(8,128)(2,1)} %get-tuple-element.29.gu_hbm, bf16[1024,3584]{1,0:T(8,128)(2,1)} %get-tuple-element.30.down_hbm, ...), custom_call_target="tpu_custom_call", output_to_operand_aliasing={{}: (4, {})} | custom-call | flops 11274289152 | bytes 29360128 | tf_op jit(solution)/shard_map/run_expert/pallas_call | solution.py:230
  295.3 0.0 copy-start.2
  295.3 0.0 copy-start.1
  295.4 116.0 %all_to_all.21.x_ref = bf16[64,8,8960]{2,1,0:T(8,128)(2,1)S(1)} all-to-all(bf16[64,8,8960]{2,1,0:T(8,128)(2,1)} %run_expert.1), channel_id=1, replica_groups={{0,2,4,6,8,10,12,14,16,18,20,22,24,26,28,30,32,34,36,38,40,42,44,46,48,..., dimensions={0} | all-to-all | bytes 18350080 | tf_op jit(solution)/shard_map/all_to_all | solution.py:340
  411.4 0.0 copy-done.2
  411.4 5.9 %combine.1 = (bf16[128,3584]{1,0:T(8,128)(2,1)}, f32[64,128]{1,0:T(8,128)S(1)}) custom-call(bf16[64,8,8960]{2,1,0:T(8,128)(2,1)S(1)} %all_to_all.21.x_ref, s32[64,128]{1,0:T(8,128)S(1)} %fusion.5.rank_ref, f32[64,128]{1,0:T(8,128)S(1)} %select_reduce_fusion.1.gate_ref, bf16[128,3584]{1,0:T(8,128)(2,1)S(1)} %copy-done.2), custom_call_target="tpu_custom_call" | custom-call | flops 2818572288 | bytes 11010048 | tf_op jit(solution)/shard_map/combine/pallas_call | solution.py:298
  417.3 0.6 select_reduce_fusion
  417.9 0.0 copy-done.1
  (10 shorter events, 0.1 us)
Async XLA Ops:
  0.6 37.3 %copy-start = (bf16[128,3584]{1,0:T(8,128)(2,1)S(1)}, bf16[128,3584]{1,0:T(8,128)(2,1)}, u32[]{:S(2)}) copy-start(bf16[128,3584]{1,0:T(8,128)(2,1)} %param.9) | copy-start | bytes 2752516
  0.6 12.0 %copy-start.6 = (bf16[128,8]{0,1:T(8,128)(2,1)S(1)}, bf16[128,8]{0,1:T(8,128)(2,1)}, u32[]{:S(2)}) copy-start(bf16[128,8]{0,1:T(8,128)(2,1)} %param.12) | copy-start | bytes 6148
  0.7 12.0 %copy-start.7 = (s32[64]{0:T(128)S(1)}, s32[64]{0:T(128)}, u32[]{:S(2)}) copy-start(s32[64]{0:T(128)} %param.13) | copy-start | bytes 772
  0.7 12.0 %copy-start.5 = (s32[128,8]{0,1:T(8,128)S(1)}, s32[128,8]{0,1:T(8,128)}, u32[]{:S(2)}) copy-start(s32[128,8]{0,1:T(8,128)} %param.11) | copy-start | bytes 12292
  0.7 12.5 %copy-start.4 = (f32[64,8,28]{0,1,2:T(8,128)S(1)}, f32[64,8,28]{0,1,2:T(8,128)}, u32[]{:S(2)}) copy-start(f32[64,8,28]{0,1,2:T(8,128)} %param.17) | copy-start | bytes 172036
  0.7 12.9 %copy-start.3 = (f32[64,28,16]{0,2,1:T(8,128)S(1)}, f32[64,28,16]{0,2,1:T(8,128)}, u32[]{:S(2)}) copy-start(f32[64,28,16]{0,2,1:T(8,128)} %param.15) | copy-start | bytes 344068
  0.7 58.3 %all-to-all-start = ((bf16[64,8,3584]{2,1,0:T(8,128)(2,1)}), bf16[64,8,3584]{2,1,0:T(8,128)(2,1)}, u32[]{:S(2)}, u32[]{:S(2)}) async-start(bf16[64,8,3584]{2,1,0:T(8,128)(2,1)} %param.16), calls=%async_computation | async-start | bytes 7340032 | tf_op jit(solution)/shard_map/all_to_all | solution.py:340
  221.5 17.3 %collective-permute-start = (bf16[64,8,7168]{2,1,0:T(8,128)(2,1)}, bf16[64,8,7168]{2,1,0:T(8,128)(2,1)}, u32[]{:S(2)}, u32[]{:S(2)}) collective-permute-start(bf16[64,8,7168]{2,1,0:T(8,128)(2,1)} %slice.19), channel_id=1, source_target_pairs={{0,1},{1,0},{2,3},{3,2},{4,5},{5,4},{6,7},{7,6},{8,9},{9,8},{10,11... | collective-permute-start | bytes 22020104 | tf_op jit(solution)/shard_map/ppermute | solution.py:388
  221.5 17.2 %collective-permute-start.1 = (bf16[64,8,3584]{2,1,0:T(8,128)(2,1)}, bf16[64,8,3584]{2,1,0:T(8,128)(2,1)}, u32[]{:S(2)}, u32[]{:S(2)}) collective-permute-start(bf16[64,8,3584]{2,1,0:T(8,128)(2,1)} %all-to-all-done.own_down), channel_id=1, source_target_pairs={{0,1},{1,0},{2,3},{3,2},{4,5},{5,4},{6,7},{7,6},{8,9},{9,8},{10,11... | collective-permute-start | bytes 11010056 | tf_op jit(solution)/shard_map/ppermute | solution.py:387
  222.0 55.0 %all-to-all-start.2 = ((bf16[64,8,3584]{2,1,0:T(8,128)(2,1)}), bf16[64,8,3584]{2,1,0:T(8,128)(2,1)}, u32[]{:S(2)}, u32[]{:S(2)}) async-start(bf16[64,8,3584]{2,1,0:T(8,128)(2,1)} %fusion.3), calls=%async_computation.2 | async-start | bytes 7340032 | tf_op jit(solution)/shard_map/all_to_all | solution.py:340
  295.3 116.0 %copy-start.2 = (bf16[128,3584]{1,0:T(8,128)(2,1)S(1)}, bf16[128,3584]{1,0:T(8,128)(2,1)}, u32[]{:S(2)}) copy-start(bf16[128,3584]{1,0:T(8,128)(2,1)} %cotangent_ref.1) | copy-start | bytes 2752516
  295.3 122.6 %copy-start.1 = (bf16[128,3584]{1,0:T(8,128)(2,1)S(1)}, bf16[128,3584]{1,0:T(8,128)(2,1)}, u32[]{:S(2)}) copy-start(bf16[128,3584]{1,0:T(8,128)(2,1)} %param.9) | copy-start | bytes 2752516
